TPU v7x, 32 devices: a whole 2x2x4 slice. The times are simulated.
32 devices in a mesh: tok: 8 (over z, core), tp: 4 (over y, x).
Axes of the slice: x: 2, y: 2, z: 4, core: 2. Of those that a mesh axis runs over, the one named last changes fastest.
Arguments:
- hidden_states: bfloat16 [16384, 1024], P(('tok', 'tp')), may hold values from -40 to 40
- first_gain: float32 [1024], replicated, may hold values from 0.1 to 1.9
- second_gain: float32 [1024], replicated, may hold values from 0.1 to 1.9
- w_query: bfloat16 [1024, 1024], P(None, 'tp'), may hold values from -1 to 1
- w_keyval: bfloat16 [1024, 1024], replicated, may hold values from -0.375 to 0.375
- w_out: bfloat16 [1024, 1024], P('tp'), may hold values from -0.75 to 0.75
- kv_cache: bfloat16 [192, 128, 1024], P('tok'), may hold values from -310 to 310
- page_table: int32 [16, 16], P('tok'), may hold values from 0 to 191, as said below
- cached_len: int32 [16], P('tok'), may hold values from 128 to 2048, as said below
- expert_ids: int32 [16384, 8], P(('tok', 'tp')), may hold values from 0 to 31, all different within a row; in each aligned block of 512 rows (0 to 511, 512 to 1023, ...) at most 256 rows name the same one
- gate_weights: float32 [16384, 8], P(('tok', 'tp')), may hold values from 0.1 to 1
- w_gate_up: bfloat16 [32, 1024, 1024], P('tp', 'tok'), may hold values from -0.1875 to 0.1875
- w_down: bfloat16 [32, 512, 1024], P('tp', 'tok'), may hold values from -1 to 1
Outputs:
- layer_out: bfloat16 [16384, 1024], P(('tok', 'tp'))
Inputs may be any that keep to these rules, and one draw needn't show every extreme that they name: `page_table`: request r's entries are pages of its own tok index, rows 24 * (r // 2) to 24 * (r // 2 + 1) - 1; its first 8 entries are the same for all requests of that tok index, and all other entries name pages that no other entry names. `cached_len`: some request has exactly 2048 cached tokens. `expert_ids`: in the rows of one device (aligned blocks of 512 rows) no expert is named by more than 256 rows, and a row names 8 different experts.
All inputs are finite; a program needn't handle non-finite values.
Results may differ from a plain program's by a relative error of at most 0.017.
The roundings to bfloat16 on the way count: a program that leaves them out, or rounds other values in their place, can miss the bound.
Values may be sent and summed in bfloat16 or wider, within the bound.
A program may use at most 128 MiB of HBM per device.

v0:
```python
import jax
import jax.numpy as jnp
from jax import lax
from jax.sharding import PartitionSpec as P

D = 1024
HEADS = 16
KV_HEADS = 8
HEAD_DIM = 64
EXPERTS = 32
FF_EXPERT = 512
TOP = 8
NEW = 1024
MAX_CACHED = 2048
REQ_DEV = 2


ATTN_SCALE = 0.015625
EPSILON = 1e-06
THETA = 10000.0


def rms_norm(values, gain):
    wide = values.astype(jnp.float32)
    factor = lax.rsqrt(jnp.mean(wide * wide, axis=-1, keepdims=True) + EPSILON)
    return (wide * factor * gain).astype(jnp.bfloat16)


def rotate(values, positions):
    row_count = values.shape[0]
    shaped = values.reshape(row_count, -1, HEAD_DIM)
    half_dim = HEAD_DIM // 2
    exponent = jnp.arange(half_dim).astype(jnp.float32) * (2.0 / HEAD_DIM)
    frequency = jnp.power(THETA, -exponent)
    angles = positions.astype(jnp.float32)[:, None] * frequency[None, :]
    cosine = jnp.cos(angles)[:, None, :]
    sine_part = jnp.sin(angles)[:, None, :]
    leading = shaped[..., :half_dim]
    trailing = shaped[..., half_dim:]
    turned = jnp.concatenate(
        [leading * cosine - trailing * sine_part, trailing * cosine + leading * sine_part], axis=-1
    )
    return turned.reshape(row_count, -1)


def attend_request(queries, keys_total, values_total, length):
    block_rows = min(NEW, 512)
    key_index = jnp.arange(MAX_CACHED + NEW, dtype=jnp.int32)

    def one_block(block_start):
        block_query = lax.dynamic_slice_in_dim(queries, block_start, block_rows, 0)
        scores = (
            jnp.einsum(
                "qgpd,kgd->gpqk", block_query, keys_total, preferred_element_type=jnp.float32
            )
            * ATTN_SCALE
        )
        query_pos = block_start + jnp.arange(block_rows, dtype=jnp.int32)
        allowed = jnp.where(
            key_index[None, :] < MAX_CACHED,
            key_index[None, :] < length,
            key_index[None, :] - MAX_CACHED <= query_pos[:, None],
        )
        scores = jnp.where(allowed, scores, -1e30)
        top_score = jnp.max(scores, axis=-1, keepdims=True)
        weights = jnp.exp(scores - top_score)
        probs = (weights / jnp.sum(weights, axis=-1, keepdims=True)).astype(jnp.bfloat16)
        mixed = jnp.einsum(
            "gpqk,kgd->qgpd", probs, values_total, preferred_element_type=jnp.float32
        )
        return mixed.astype(jnp.bfloat16).reshape(block_rows, -1)

    starts = jnp.arange(NEW // block_rows, dtype=jnp.int32) * block_rows
    return lax.map(one_block, starts).reshape(NEW, -1)


def shards(
    hidden_states,
    first_gain,
    second_gain,
    w_query,
    w_keyval,
    w_out,
    kv_cache,
    page_table,
    cached_len,
    expert_ids,
    gate_weights,
    w_gate_up,
    w_down,
):
    gate_up_full, down_full = (
        lax.all_gather(w_gate_up, "tok", axis=1, tiled=True),
        lax.all_gather(w_down, "tok", axis=1, tiled=True),
    )
    tok_rows = hidden_states.shape[0]
    tp_size = lax.axis_size("tp")
    tp_rank = lax.axis_index("tp")
    local_heads = HEADS // tp_size
    group_size = HEADS // KV_HEADS
    local_kv = max(local_heads // group_size, 1)
    per_group = local_heads // local_kv
    head_width = local_heads * HEAD_DIM
    kv_width = local_kv * HEAD_DIM
    kv_cols = KV_HEADS * HEAD_DIM
    group_tokens = REQ_DEV * NEW
    first_kv = tp_rank * local_heads // group_size
    request_range = jnp.arange(REQ_DEV, dtype=jnp.int32)
    normed = rms_norm(hidden_states, first_gain)
    key_part = lax.dynamic_slice_in_dim(w_keyval, first_kv * HEAD_DIM, kv_width, 1)
    value_part = lax.dynamic_slice_in_dim(w_keyval, kv_cols + first_kv * HEAD_DIM, kv_width, 1)
    piece = lax.all_gather(normed, "tp", axis=0, tiled=True)
    row_index = jnp.arange(piece.shape[0], dtype=jnp.int32)
    owner = row_index // NEW
    base_len = jnp.sum(
        jnp.where(owner[:, None] == request_range[None, :], cached_len[None, :], 0), axis=1
    )
    piece_pos = base_len + row_index % NEW
    query_rows = rotate(jnp.dot(piece, w_query, preferred_element_type=jnp.float32), piece_pos)
    key_rows = rotate(jnp.dot(piece, key_part, preferred_element_type=jnp.float32), piece_pos)
    value_rows = jnp.dot(piece, value_part, preferred_element_type=jnp.float32)
    projected = jnp.concatenate([query_rows, key_rows, value_rows], axis=1).astype(jnp.bfloat16)
    queries = projected[:, :head_width].reshape(REQ_DEV, NEW, local_kv, per_group, HEAD_DIM)
    new_keys = projected[:, head_width : head_width + kv_width].reshape(
        REQ_DEV, NEW, local_kv, HEAD_DIM
    )
    new_values = projected[:, head_width + kv_width :].reshape(REQ_DEV, NEW, local_kv, HEAD_DIM)
    cache_keys = lax.dynamic_slice_in_dim(kv_cache, first_kv * HEAD_DIM, kv_width, 2)
    cache_values = lax.dynamic_slice_in_dim(kv_cache, kv_cols + first_kv * HEAD_DIM, kv_width, 2)
    local_pages = page_table - lax.axis_index("tok") * kv_cache.shape[0]

    def per_request(inputs):
        page_ids, length, request_q, request_k, request_v = inputs
        keys_total = jnp.concatenate(
            [
                jnp.take(cache_keys, page_ids, axis=0).reshape(MAX_CACHED, local_kv, HEAD_DIM),
                request_k,
            ],
            axis=0,
        )
        values_total = jnp.concatenate(
            [
                jnp.take(cache_values, page_ids, axis=0).reshape(MAX_CACHED, local_kv, HEAD_DIM),
                request_v,
            ],
            axis=0,
        )
        return attend_request(request_q, keys_total, values_total, length)

    attended = lax.map(
        per_request, (local_pages, cached_len, queries, new_keys, new_values)
    ).reshape(group_tokens, head_width)
    projected_out = lax.psum_scatter(
        jnp.dot(attended, w_out, preferred_element_type=jnp.float32),
        "tp",
        scatter_dimension=0,
        tiled=True,
    )
    middle = (hidden_states.astype(jnp.float32) + projected_out).astype(jnp.bfloat16)
    normed_two = rms_norm(middle, second_gain)
    experts_local = EXPERTS // tp_size
    capacity = 2 * tok_rows * TOP // EXPERTS
    expert_range = jnp.arange(EXPERTS, dtype=jnp.int32)
    onehot = (expert_ids[:, :, None] == expert_range[None, None, :]).astype(jnp.int32)
    per_token = jnp.sum(onehot, axis=1)
    earlier = jnp.cumsum(per_token, axis=0) - per_token
    slot_ids = jnp.sum(onehot * earlier[:, None, :], axis=2)
    target = expert_ids * capacity + slot_ids
    outgoing_rows = jnp.broadcast_to(normed_two[:, None, :], (tok_rows, TOP, D))
    send_buffer = jnp.zeros((EXPERTS * capacity, D), jnp.bfloat16).at[target].set(outgoing_rows)
    received = lax.all_to_all(
        send_buffer.reshape(tp_size, experts_local, capacity, D),
        "tp",
        split_axis=0,
        concat_axis=2,
        tiled=True,
    )
    received = received.reshape(experts_local, tp_size * capacity, D)
    both = jnp.einsum("esd,edf->esf", received, gate_up_full, preferred_element_type=jnp.float32)
    activated = (jax.nn.silu(both[..., :FF_EXPERT]) * both[..., FF_EXPERT:]).astype(jnp.bfloat16)
    produced = jnp.einsum(
        "esf,efd->esd", activated, down_full, preferred_element_type=jnp.float32
    ).astype(jnp.bfloat16)
    returned = lax.all_to_all(
        produced.reshape(experts_local, tp_size, capacity, D),
        "tp",
        split_axis=1,
        concat_axis=0,
        tiled=True,
    )
    returned = returned.reshape(EXPERTS * capacity, D)
    picked = returned[target]
    mixture = jnp.einsum("tk,tkd->td", gate_weights, picked.astype(jnp.float32))
    return (middle.astype(jnp.float32) + mixture).astype(jnp.bfloat16)


def solution(mesh):
    in_specs = (
        P(("tok", "tp"), None),
        P(),
        P(),
        P(None, "tp"),
        P(),
        P("tp", None),
        P("tok", None, None),
        P("tok", None),
        P("tok"),
        P(("tok", "tp"), None),
        P(("tok", "tp"), None),
        P("tp", "tok", None),
        P("tp", "tok", None),
    )
    out_specs = P(("tok", "tp"), None)
    return jax.shard_map(shards, mesh=mesh, in_specs=in_specs, out_specs=out_specs, check_vma=False)
```

profile of v0, /device:TPU:0, one launch (start us, length us, event | category | flops | bytes accessed | tf_op | source)
XLA Modules:
  0.0 854.8 jit_solution(3257737968800533911)
XLA Ops:
  7.4 1.7 fusion.42
  9.0 2.5 fusion.44
  11.7 0.7 fusion.54
  12.5 3.7 constant_dynamic-slice_fusion.1
  16.1 1.3 broadcast_subtract_fusion
  17.4 1.0 multiply_cosine_fusion
  18.4 48.8 %all-gather.4.cloned.1.call-done = bf16[2048,1024]{1,0:T(8,128)(2,1)} async-done(((bf16[512,1024]{1,0:T(8,128)(2,1)}), bf16[2048,1024]{1,0:T(8,128)(2,1)}) %all-gather.4.cloned.1.call-update) | async-done | bytes 4194320 | tf_op jit(solution)/shard_map/all_gather | solution.py:112
  67.1 3.9 fusion.51
  71.3 0.8 copy.75
  72.1 1.3 convolution_convert_fusion.1
  73.9 1.9 copy.54
  75.7 3.6 fusion.77
  79.7 0.8 reshape.193
  80.5 1.3 copy.52
  81.9 143.1 %while.34 = (s32[]{:T(128)}, bf16[2,1024,256]{2,1,0:T(8,128)(2,1)}, bf16[2,1024,2,2,64]{1,4,3,2,0:T(8,128)(2,1)}, s32[2,16]{1,0:T(2,128)}, bf16[24,128,128]{2,1,...) while((s32[]{:T(128)}, bf16[2,1024,256]{2,1,0:T(8,128)(2,1)}, ...), condition=%wide.region_7.9_spmd, body=%wide.region_2.8_spmd.sunk | while | flops 1655322240 | bytes 75560320 | solution.py:150
  82.0 0.7 compare_and_fusion.2
  82.7 1.8 gather_fusion
  84.5 1.8 gather_fusion.1
  87.1 1.1 dynamic-slice_bitcast_fusion.6
  88.9 0.9 pad_maximum_fusion.7
  89.9 1.1 dynamic-slice_bitcast_fusion.5
  91.5 60.1 %while.35 = (s32[]{:T(128)}, bf16[2,512,256]{2,1,0:T(8,128)(2,1)}, s32[]{:T(128)}, s32[2]{0:T(128)S(1)}, bf16[1024,2,2,64]{0,3,2,1:T(8,128)(2,1)S(1)}, /*index=5...) while((s32[]{:T(128)}, bf16[2,512,256]{2,1,0:T(8,128)(2,1)}, ...), condition=%wide.region_6.7_spmd.clone.clone, body=%wide.region_3.6_spmd.clone.clone.sunk | while | flops 1651651072 | bytes 60874968 | solution.py:74
  94.0 0.6 iota_add_fusion.5
  95.2 1.1 compare_select_fusion.6
  96.4 13.6 %fusion.99 = (f32[2,2,512]{2,1,0:T(2,128)S(1)}, f32[2,2,512,3072]{3,2,1,0:T(8,128)}) fusion(pred[512,3072]{1,0:T(8,128)(4,1)S(1)} %compare_select_fusion.6, bf16[3072,2,64]{0,2,1:T(8,128)(2,1)S(1)} %get-tuple-element.528, bf16[1024,2,2,64]{0,3,2,1:T(8,128)(2,1)S(1)} %get-tuple-element.527, s32[]{:T(128)S(6)} %select_n.125), kind=kOutput, calls=%fused_computation.119.clone.1 | convolution fusion | flops 830475264 | bytes 27795460 | tf_op jit(solution)/shard_map/while/body/eval_jaxpr/while/body/eval_jaxpr/sub | solution.py:66
  110.0 10.6 %fusion.100 = bf16[2,2,512,64]{2,3,1,0:T(8,128)(2,1)S(1)} fusion(f32[2,2,512,3072]{3,2,1,0:T(8,128)} %get-tuple-element.501, f32[2,2,512]{2,1,0:T(2,128)S(1)} %get-tuple-element.502, bf16[3072,2,64]{0,2,1:T(8,128)(2,1)} %get-tuple-element.529), kind=kOutput, calls=%fused_computation.18.clone.1 | convolution fusion | flops 818020352 | bytes 26222592 | tf_op jit(solution)/shard_map/while/body/eval_jaxpr/while/body/eval_jaxpr/gpqk,kgd->qgpd/dot_general | solution.py:68
  120.8 0.8 copy-done.4
  125.2 1.1 compare_select_fusion.6
  126.4 13.6 %fusion.99 = (f32[2,2,512]{2,1,0:T(2,128)S(1)}, f32[2,2,512,3072]{3,2,1,0:T(8,128)}) fusion(pred[512,3072]{1,0:T(8,128)(4,1)S(1)} %compare_select_fusion.6, bf16[3072,2,64]{0,2,1:T(8,128)(2,1)S(1)} %get-tuple-element.528, bf16[1024,2,2,64]{0,3,2,1:T(8,128)(2,1)S(1)} %get-tuple-element.527, s32[]{:T(128)S(6)} %select_n.125), kind=kOutput, calls=%fused_computation.119.clone.1 | convolution fusion | flops 830475264 | bytes 27795460 | tf_op jit(solution)/shard_map/while/body/eval_jaxpr/while/body/eval_jaxpr/sub | solution.py:66
  140.0 10.6 %fusion.100 = bf16[2,2,512,64]{2,3,1,0:T(8,128)(2,1)S(1)} fusion(f32[2,2,512,3072]{3,2,1,0:T(8,128)} %get-tuple-element.501, f32[2,2,512]{2,1,0:T(2,128)S(1)} %get-tuple-element.502, bf16[3072,2,64]{0,2,1:T(8,128)(2,1)} %get-tuple-element.529), kind=kOutput, calls=%fused_computation.18.clone.1 | convolution fusion | flops 818020352 | bytes 26222592 | tf_op jit(solution)/shard_map/while/body/eval_jaxpr/while/body/eval_jaxpr/gpqk,kgd->qgpd/dot_general | solution.py:68
  150.8 0.8 copy-done.4
  151.6 1.9 bitcast_dynamic-update-slice_fusion.2
  153.5 0.7 compare_and_fusion.2
  154.2 1.8 gather_fusion
  156.0 1.8 gather_fusion.1
  158.6 1.1 dynamic-slice_bitcast_fusion.6
  160.4 0.9 pad_maximum_fusion.7
  161.3 1.1 dynamic-slice_bitcast_fusion.5
  163.0 60.1 %while.35 = (s32[]{:T(128)}, bf16[2,512,256]{2,1,0:T(8,128)(2,1)}, s32[]{:T(128)}, s32[2]{0:T(128)S(1)}, bf16[1024,2,2,64]{0,3,2,1:T(8,128)(2,1)S(1)}, /*index=5...) while((s32[]{:T(128)}, bf16[2,512,256]{2,1,0:T(8,128)(2,1)}, ...), condition=%wide.region_6.7_spmd.clone.clone, body=%wide.region_3.6_spmd.clone.clone.sunk | while | flops 1651651072 | bytes 60874968 | solution.py:74
  166.7 1.1 compare_select_fusion.6
  167.8 13.6 %fusion.99 = (f32[2,2,512]{2,1,0:T(2,128)S(1)}, f32[2,2,512,3072]{3,2,1,0:T(8,128)}) fusion(pred[512,3072]{1,0:T(8,128)(4,1)S(1)} %compare_select_fusion.6, bf16[3072,2,64]{0,2,1:T(8,128)(2,1)S(1)} %get-tuple-element.528, bf16[1024,2,2,64]{0,3,2,1:T(8,128)(2,1)S(1)} %get-tuple-element.527, s32[]{:T(128)S(6)} %select_n.125), kind=kOutput, calls=%fused_computation.119.clone.1 | convolution fusion | flops 830475264 | bytes 27795460 | tf_op jit(solution)/shard_map/while/body/eval_jaxpr/while/body/eval_jaxpr/sub | solution.py:66
  181.4 10.6 %fusion.100 = bf16[2,2,512,64]{2,3,1,0:T(8,128)(2,1)S(1)} fusion(f32[2,2,512,3072]{3,2,1,0:T(8,128)} %get-tuple-element.501, f32[2,2,512]{2,1,0:T(2,128)S(1)} %get-tuple-element.502, bf16[3072,2,64]{0,2,1:T(8,128)(2,1)} %get-tuple-element.529), kind=kOutput, calls=%fused_computation.18.clone.1 | convolution fusion | flops 818020352 | bytes 26222592 | tf_op jit(solution)/shard_map/while/body/eval_jaxpr/while/body/eval_jaxpr/gpqk,kgd->qgpd/dot_general | solution.py:68
  192.2 0.8 copy-done.4
  196.7 1.1 compare_select_fusion.6
  197.9 13.6 %fusion.99 = (f32[2,2,512]{2,1,0:T(2,128)S(1)}, f32[2,2,512,3072]{3,2,1,0:T(8,128)}) fusion(pred[512,3072]{1,0:T(8,128)(4,1)S(1)} %compare_select_fusion.6, bf16[3072,2,64]{0,2,1:T(8,128)(2,1)S(1)} %get-tuple-element.528, bf16[1024,2,2,64]{0,3,2,1:T(8,128)(2,1)S(1)} %get-tuple-element.527, s32[]{:T(128)S(6)} %select_n.125), kind=kOutput, calls=%fused_computation.119.clone.1 | convolution fusion | flops 830475264 | bytes 27795460 | tf_op jit(solution)/shard_map/while/body/eval_jaxpr/while/body/eval_jaxpr/sub | solution.py:66
  211.5 10.6 %fusion.100 = bf16[2,2,512,64]{2,3,1,0:T(8,128)(2,1)S(1)} fusion(f32[2,2,512,3072]{3,2,1,0:T(8,128)} %get-tuple-element.501, f32[2,2,512]{2,1,0:T(2,128)S(1)} %get-tuple-element.502, bf16[3072,2,64]{0,2,1:T(8,128)(2,1)} %get-tuple-element.529), kind=kOutput, calls=%fused_computation.18.clone.1 | convolution fusion | flops 818020352 | bytes 26222592 | tf_op jit(solution)/shard_map/while/body/eval_jaxpr/while/body/eval_jaxpr/gpqk,kgd->qgpd/dot_general | solution.py:68
  222.2 0.8 copy-done.4
  223.1 1.9 bitcast_dynamic-update-slice_fusion.2
  224.9 5.8 fusion.78
  231.5 1.4 reduce-window.6
  233.6 83.8 %reduce-scatter.2.cloned.1.call-done = f32[512,1024]{1,0:T(8,128)} async-done(((f32[2048,1024]{1,0:T(8,128)}), f32[512,1024]{1,0:T(8,128)}) %reduce-scatter.2.cloned.1.call-update) | async-done | bytes 2097168 | tf_op jit(solution)/shard_map/reduce_scatter | solution.py:153
  317.4 2.0 fusion.46
  319.7 28.2 %scatter_custom_fusion = bf16[8192,1024]{1,0:T(8,128)(2,1)} fusion(s32[4096]{0:T(1024)S(1)} %reshape.230, bf16[]{:T(256)} %constant.163.clone.1, bf16[512,1024]{1,0:T(8,128)(2,1)S(1)} %fusion.48), kind=kCustom, calls=%fused_computation.53 | custom fusion | bytes 17825794 | tf_op jit(solution)/shard_map/scatter | solution.py:170
  348.0 7.0 all-to-all-start
  355.5 181.9 %all-to-all-done = bf16[4,8,256,1024]{3,2,1,0:T(8,128)(2,1)} async-done(((bf16[4,8,256,1024]{3,2,1,0:T(8,128)(2,1)}), bf16[4,8,256,1024]{3,2,1,0:T(8,128)(2,1)}, u32[]{:S(2)}, u32[]{:S(2)}) %all-to-all-start) | async-done | bytes 16777248 | tf_op jit(solution)/shard_map/all_to_all | solution.py:171
  537.5 13.8 %copy.58 = bf16[1,8,4,256,1024]{4,3,2,1,0:T(8,128)(2,1)} copy(bf16[1,8,4,256,1024]{4,3,1,2,0:T(8,128)(2,1)} %bitcast.14) | data formatting | bytes 33554432 | tf_op jit(solution)/shard_map/all_to_all | solution.py:171
  551.3 30.0 %fusion.79 = f32[8,1024,1024]{2,1,0:T(8,128)} fusion(bf16[8,1024,1024]{2,1,0:T(8,128)(2,1)} %bitcast.130, bf16[8,1024,1024]{2,1,0:T(8,128)(2,1)} %all-gather.6.cloned.1.call-done), kind=kOutput, calls=%fused_computation.122 | convolution fusion | flops 17179869184 | bytes 67108864 | tf_op jit(solution)/shard_map/esd,edf->esf/dot_general | solution.py:179
  581.4 23.8 %convolution_convert_fusion = bf16[8,1024,1024]{2,1,0:T(8,128)(2,1)} fusion(bf16[8,512,1024]{2,1,0:T(8,128)(2,1)} %all-gather.8.cloned.1.call-done, f32[8,1024,1024]{2,1,0:T(8,128)} %fusion.79), kind=kOutput, calls=%fused_computation.50 | convolution fusion | flops 8623489024 | bytes 58720256 | tf_op jit(solution)/shard_map/esf,efd->esd/dot_general | solution.py:181
  605.2 13.9 %copy.59 = bf16[8,4,256,1024]{3,2,0,1:T(8,128)(2,1)} copy(bf16[8,4,256,1024]{3,2,1,0:T(8,128)(2,1)} %bitcast.131) | data formatting | bytes 33554432 | tf_op jit(solution)/shard_map/reshape | solution.py:185
  619.0 7.3 all-to-all-start.1
  626.6 181.4 %all-to-all-done.1 = bf16[8,4,256,1024]{3,2,0,1:T(8,128)(2,1)} async-done(((bf16[8,4,256,1024]{3,2,0,1:T(8,128)(2,1)}), bf16[8,4,256,1024]{3,2,0,1:T(8,128)(2,1)}, u32[]{:S(2)}, u32[]{:S(2)}) %all-to-all-start.1) | async-done | bytes 16777248 | tf_op jit(solution)/shard_map/all_to_all | solution.py:184
  808.0 29.0 %gather_fusion.2 = bf16[4096,1024]{1,0:T(8,128)(2,1)} fusion(bf16[8192,1024]{1,0:T(8,128)(2,1)} %bitcast.19, s32[4096]{0:T(1024)S(1)} %broadcast_clamp_fusion), kind=kCustom, calls=%fused_computation.2 | custom fusion | bytes 16793600 | tf_op jit(solution)/shard_map/gather | solution.py:192
  837.0 7.0 fusion.35
  844.0 3.1 fusion.49
  (109 shorter events, 15.0 us)
Async XLA Ops:
  7.4 59.8 %copy-start = (bf16[1024,1024]{1,0:T(8,128)(2,1)S(1)}, bf16[1024,1024]{1,0:T(8,128)(2,1)}, u32[]{:S(2)}) copy-start(bf16[1024,1024]{1,0:T(8,128)(2,1)} %param.23) | copy-start | bytes 6291460
  7.4 59.8 %all-gather.4.cloned.1.call-start = ((), (), s32[]{:S(2)}) async-start(), calls=%async_computation.3 | async-start | bytes 5242880 | tf_op jit(solution)/shard_map/all_gather | solution.py:112
  11.6 305.8 %reduce-scatter.2.cloned.1.call-start = ((), (), s32[]{:S(2)}) async-start(), calls=%async_computation.4 | async-start | bytes 10485760 | tf_op jit(solution)/shard_map/reduce_scatter | solution.py:153
  67.1 5.0 copy-start.2
  75.7 6.1 copy-start.9
  91.5 61.9 %copy-start.10 = (s32[2]{0:T(128)S(1)}, s32[2]{0:T(128)}, u32[]{:S(2)}) copy-start(s32[2]{0:T(128)} %get-tuple-element.607) | copy-start | bytes 28 | tf_op jit(solution)/shard_map/while
  110.0 10.7 %copy-start.3 = (bf16[2,512,256]{2,1,0:T(8,128)(2,1)S(1)}, bf16[2,512,256]{2,1,0:T(8,128)(2,1)}, u32[]{:S(2)}) copy-start(bf16[2,512,256]{2,1,0:T(8,128)(2,1)} %get-tuple-element.514) | copy-start | bytes 1572868 | tf_op jit(solution)/shard_map/while/body/eval_jaxpr/while
  120.7 0.8 copy-start.4
  140.0 10.7 %copy-start.3 = (bf16[2,512,256]{2,1,0:T(8,128)(2,1)S(1)}, bf16[2,512,256]{2,1,0:T(8,128)(2,1)}, u32[]{:S(2)}) copy-start(bf16[2,512,256]{2,1,0:T(8,128)(2,1)} %get-tuple-element.514) | copy-start | bytes 1572868 | tf_op jit(solution)/shard_map/while/body/eval_jaxpr/while
  150.8 0.8 copy-start.4
  163.0 61.9 %copy-start.10 = (s32[2]{0:T(128)S(1)}, s32[2]{0:T(128)}, u32[]{:S(2)}) copy-start(s32[2]{0:T(128)} %get-tuple-element.607) | copy-start | bytes 28 | tf_op jit(solution)/shard_map/while
  181.4 10.7 %copy-start.3 = (bf16[2,512,256]{2,1,0:T(8,128)(2,1)S(1)}, bf16[2,512,256]{2,1,0:T(8,128)(2,1)}, u32[]{:S(2)}) copy-start(bf16[2,512,256]{2,1,0:T(8,128)(2,1)} %get-tuple-element.514) | copy-start | bytes 1572868 | tf_op jit(solution)/shard_map/while/body/eval_jaxpr/while
  192.2 0.8 copy-start.4
  211.5 10.7 %copy-start.3 = (bf16[2,512,256]{2,1,0:T(8,128)(2,1)S(1)}, bf16[2,512,256]{2,1,0:T(8,128)(2,1)}, u32[]{:S(2)}) copy-start(bf16[2,512,256]{2,1,0:T(8,128)(2,1)} %get-tuple-element.514) | copy-start | bytes 1572868 | tf_op jit(solution)/shard_map/while/body/eval_jaxpr/while
  222.2 0.8 copy-start.4
  224.9 6.5 copy-start.6
  230.8 86.6 %copy-start.5 = (bf16[512,1024]{1,0:T(8,128)(2,1)S(1)}, bf16[512,1024]{1,0:T(8,128)(2,1)}, u32[]{:S(2)}) copy-start(bf16[512,1024]{1,0:T(8,128)(2,1)} %param.19) | copy-start | bytes 3145732
  230.8 88.6 %copy-start.8 = (f32[1024]{0:T(1024)S(1)}, f32[1024]{0:T(1024)}, u32[]{:S(2)}) copy-start(f32[1024]{0:T(1024)} %param.21) | copy-start | bytes 12292
  230.8 320.5 %all-gather.6.cloned.1.call-start = ((), (), s32[]{:S(2)}) async-start(), calls=%async_computation.5 | async-start | bytes 18874368 | tf_op jit(solution)/shard_map/all_gather | solution.py:93
  348.0 189.5 %all-to-all-start = ((bf16[4,8,256,1024]{3,2,1,0:T(8,128)(2,1)}), bf16[4,8,256,1024]{3,2,1,0:T(8,128)(2,1)}, u32[]{:S(2)}, u32[]{:S(2)}) async-start(bf16[4,8,256,1024]{3,2,1,0:T(8,128)(2,1)} %bitcast.129), calls=%async_computation.1 | async-start | bytes 33554432 | tf_op jit(solution)/shard_map/all_to_all | solution.py:171
  355.0 226.4 %all-gather.8.cloned.1.call-start = ((), (), s32[]{:S(2)}) async-start(), calls=%async_computation.6 | async-start | bytes 9437184 | tf_op jit(solution)/shard_map/all_gather | solution.py:94
  619.0 7.3 copy-start.7
  619.0 189.0 %all-to-all-start.1 = ((bf16[8,4,256,1024]{3,2,0,1:T(8,128)(2,1)}), bf16[8,4,256,1024]{3,2,0,1:T(8,128)(2,1)}, u32[]{:S(2)}, u32[]{:S(2)}) async-start(bf16[8,4,256,1024]{3,2,0,1:T(8,128)(2,1)} %copy.59), calls=%async_computation.2 | async-start | bytes 33554432 | tf_op jit(solution)/shard_map/all_to_all | solution.py:184
  808.0 39.1 %copy-start.1 = (bf16[1024,1024]{1,0:T(8,128)(2,1)S(1)}, bf16[1024,1024]{1,0:T(8,128)(2,1)}, u32[]{:S(2)}) copy-start(bf16[1024,1024]{1,0:T(8,128)(2,1)} %param.23) | copy-start | bytes 6291460
Sparse Core Ops, SparseCore 0:
  11.7 55.3 all-gather.3
  230.9 86.4 reduce-scatter.1
Sparse Core Ops, SparseCore 1:
  233.0 150.9 all-gather.5
  385.5 80.1 all-gather.7
where the time goes:
time: 862 us; the launch traced here: 855 us
  waiting for transfers between devices  497 us (58%)
  matrix products  172 us (20%)
  local copies, waits for them, and re-layouts  120 us (14%)
  other arithmetic  27.9 us (3%)
  between operations  15.3 us (2%)
  starting transfers between devices  14.4 us (2%)
    all_to_all x1, waiting for transfers between devices, shards(): lax.all_to_all(send_buffer.reshape(tp_size, experts_local, capacity, D),...  182 us
    all_to_all x1, waiting for transfers between devices, shards(): lax.all_to_all(produced.reshape(experts_local, tp_size, capacity, D), 'tp...  181 us
    reduce_scatter x1, waiting for transfers between devices, shards(): lax.psum_scatter(jnp.dot(attended, w_out, preferred_element_type=jnp.floa...  83.8 us
    sub x4, matrix products, one_block(): weights = jnp.exp(scores - top_score)  54.5 us
    all_gather x1, waiting for transfers between devices, shards(): piece = lax.all_gather(normed, 'tp', axis=0, tiled=True)  48.8 us
    dot_general x4, matrix products, one_block(): jnp.einsum('gpqk,kgd->qgpd', probs, values_total, preferred_element_type=...  42.2 us
    dot_general x1, matrix products, shards(): jnp.einsum('esd,edf->esf', received, gate_up_full, preferred_element_type...  30 us
    gather x1, local copies, waits for them, and re-layouts, shards(): picked = returned[target]  29 us
  transfers between devices with their start and end apart: 6, of which 4 were waited for; matrix products, arithmetic and copies ran while one was open for 10% of the time, Pallas kernels for 0%

commit v1 on v0

v1 whole, which is shorter than its diff:
```python
import functools

import jax
import jax.numpy as jnp
from jax import lax
from jax.experimental import pallas as pl
from jax.experimental.pallas import tpu as pltpu
from jax.sharding import PartitionSpec as P

D = 1024
HEADS = 16
KV_HEADS = 8
HEAD_DIM = 64
EXPERTS = 32
FF_EXPERT = 512
TOP = 8
NEW = 1024
REQ_DEV = 2
PAGE = 128
MAX_PAGES = 16

ATTN_SCALE = 0.015625
EPSILON = 1e-06
THETA = 10000.0

LANES = 128
PAIRS = KV_HEADS // 2
KEY_BLOCK = 512
EXPERT_GROUPS = 2
NEGATIVE = -1e30
VMEM_LIMIT = 56 * 1024 * 1024


def params(*semantics):
    return pltpu.CompilerParams(
        vmem_limit_bytes=VMEM_LIMIT, dimension_semantics=semantics or None
    )


def rms_rows(wide, gain):
    factor = lax.rsqrt(jnp.mean(wide * wide, axis=-1, keepdims=True) + EPSILON)
    return (wide * factor * gain).astype(jnp.bfloat16)


def turn(values, cosine, sine):
    lane = lax.broadcasted_iota(jnp.int32, values.shape, 1)
    partner = jnp.where(
        lane % HEAD_DIM < HEAD_DIM // 2, pltpu.roll(values, 96, 1), pltpu.roll(values, 32, 1)
    )
    return values * cosine + partner * sine


def keyval_kernel(x_ref, gain_ref, w_ref, cos_ref, sin_ref, normed_ref, kv_ref):
    normed = rms_rows(x_ref[...].astype(jnp.float32), gain_ref[...])
    normed_ref[...] = normed
    for at in range(0, D, 256):
        part = jnp.dot(normed, w_ref[:, at : at + 256], preferred_element_type=jnp.float32)
        for sub in range(0, 256, LANES):
            piece = part[:, sub : sub + LANES]
            if at < KV_HEADS * HEAD_DIM:
                piece = turn(piece, cos_ref[...], sin_ref[...])
            kv_ref[:, at + sub : at + sub + LANES] = piece.astype(jnp.bfloat16)


def query_kernel(normed_ref, w_ref, cos_ref, sin_ref, q_ref):
    normed = normed_ref[...]
    for at in range(0, D, 256):
        part = jnp.dot(normed, w_ref[:, at : at + 256], preferred_element_type=jnp.float32)
        for sub in range(0, 256, LANES):
            piece = turn(part[:, sub : sub + LANES], cos_ref[...], sin_ref[...])
            piece = piece.astype(jnp.bfloat16).astype(jnp.float32) * ATTN_SCALE
            q_ref[:, at + sub : at + sub + LANES] = piece.astype(jnp.bfloat16)


def attention_kernel(
    pages_ref, sizes_ref, q_ref, ck_ref, cv_ref, nk_ref, nv_ref, o_ref, qp, top, acc
):
    rows = q_ref.shape[0]
    length = sizes_ref[0]
    first_row = sizes_ref[1]
    lane = lax.broadcasted_iota(jnp.int32, (rows, LANES), 1)
    low = lane < HEAD_DIM
    for head in range(4):
        block = q_ref[:, (head // 2) * LANES : (head // 2 + 1) * LANES].astype(jnp.float32)
        if head in (1, 2):
            block = pltpu.roll(block, HEAD_DIM, 1)
        keep = low if head < 2 else jnp.logical_not(low)
        qp[head] = jnp.where(keep, block, 0.0).astype(jnp.bfloat16)
        top[head] = jnp.full((rows, 1), NEGATIVE, jnp.float32)
        acc[head] = jnp.zeros((rows, 2 * LANES), jnp.float32)

    def update(keys, values, allowed):
        extended = jnp.concatenate([values, jnp.ones_like(values)], axis=1)
        for head in range(4):
            scores = lax.dot_general(
                qp[head], keys, (((1,), (1,)), ((), ())), preferred_element_type=jnp.float32
            )
            if allowed is not None:
                scores = jnp.where(allowed, scores, NEGATIVE)
            before = top[head]
            after = jnp.maximum(before, jnp.max(scores, axis=1, keepdims=True))
            weights = jnp.exp(scores - after).astype(jnp.bfloat16)
            top[head] = after
            acc[head] = acc[head] * jnp.exp(before - after) + jnp.dot(
                weights, extended, preferred_element_type=jnp.float32
            )

    per_block = KEY_BLOCK // PAGE

    def cached_block(index):
        ids = [pages_ref[index * per_block + i] for i in range(per_block)]
        keys = jnp.concatenate([ck_ref[page] for page in ids], axis=0)
        values = jnp.concatenate([cv_ref[page] for page in ids], axis=0)
        return keys, values

    key_index = lax.broadcasted_iota(jnp.int32, (rows, KEY_BLOCK), 1)
    full = length // KEY_BLOCK

    def full_block(index, carry):
        update(*cached_block(index), None)
        return carry

    lax.fori_loop(0, full, full_block, 0)

    @pl.when(length % KEY_BLOCK > 0)
    def _():
        update(*cached_block(full), key_index < length - full * KEY_BLOCK)

    row_index = lax.broadcasted_iota(jnp.int32, (rows, KEY_BLOCK), 0) + first_row

    def new_block(index, carry):
        at = pl.multiple_of(index * KEY_BLOCK, KEY_BLOCK)
        update(
            nk_ref[pl.ds(at, KEY_BLOCK), :],
            nv_ref[pl.ds(at, KEY_BLOCK), :],
            key_index + at <= row_index,
        )
        return carry

    lax.fori_loop(0, (first_row + rows + KEY_BLOCK - 1) // KEY_BLOCK, new_block, 0)

    out = []
    for head in range(4):
        total = acc[head]
        mixed = total[:, :LANES] / total[:, LANES:]
        if head in (1, 2):
            mixed = pltpu.roll(mixed, HEAD_DIM, 1)
        out.append(mixed)
    o_ref[:, :LANES] = jnp.where(low, out[0], out[1]).astype(jnp.bfloat16)
    o_ref[:, LANES:] = jnp.where(low, out[2], out[3]).astype(jnp.bfloat16)


def out_kernel(att_ref, w_ref, x_ref, gain_ref, mid_ref, normed_ref):
    total = jnp.dot(att_ref[...], w_ref[...], preferred_element_type=jnp.float32)
    mid = (x_ref[...].astype(jnp.float32) + total).astype(jnp.bfloat16)
    mid_ref[...] = mid
    normed_ref[...] = rms_rows(mid.astype(jnp.float32), gain_ref[...])


def expert_kernel(first, last, x_ref, gates_ref, gu_ref, down_ref, *rest):
    before_ref, out_ref, total = (None, *rest) if first else rest
    expert = pl.program_id(1)
    rows = x_ref.shape[0]
    sub = min(rows, 256)
    gate_up = gu_ref[...].reshape(D, 2 * FF_EXPERT)
    down = down_ref[...].reshape(FF_EXPERT, D)

    def one(index, carry):
        span = pl.ds(pl.multiple_of(index * sub, sub), sub)
        both = jnp.dot(x_ref[span, :], gate_up, preferred_element_type=jnp.float32)
        lane = lax.broadcasted_iota(jnp.int32, (sub, gates_ref.shape[1]), 1)
        gate = jnp.sum(jnp.where(lane == expert, gates_ref[span, :], 0.0), axis=1, keepdims=True)
        left = both[:, :FF_EXPERT]
        act = left / (1.0 + jnp.exp(-left)) * both[:, FF_EXPERT:] * gate
        made = jnp.dot(act.astype(jnp.bfloat16), down, preferred_element_type=jnp.float32)

        @pl.when(expert == 0)
        def _():
            if first:
                total[span, :] = made
            else:
                total[span, :] = before_ref[span, :].astype(jnp.float32) + made

        @pl.when(expert > 0)
        def _():
            total[span, :] += made

        return carry

    lax.fori_loop(0, rows // sub, one, 0)

    @pl.when(expert == pl.num_programs(1) - 1)
    def _():
        out_ref[...] = total[...].astype(out_ref.dtype)


def experts(rows_in, gates, gate_up, down, before, last):
    total_rows = rows_in.shape[0]
    chunk = min(total_rows, 1024)
    tok, count, depth, _ = gate_up.shape
    ff_depth = down.shape[2]
    row_block = pl.BlockSpec((chunk, D), lambda r, e: (r, 0))
    in_specs = [
        row_block,
        pl.BlockSpec((chunk, gates.shape[1]), lambda r, e: (r, 0)),
        pl.BlockSpec((tok, 1, depth, 2 * FF_EXPERT), lambda r, e: (0, e, 0, 0)),
        pl.BlockSpec((tok, 1, ff_depth, D), lambda r, e: (0, e, 0, 0)),
    ]
    operands = [rows_in, gates, gate_up, down]
    if before is not None:
        in_specs.append(row_block)
        operands.append(before)
    kind = jnp.bfloat16 if last else jnp.float32
    return pl.pallas_call(
        functools.partial(expert_kernel, before is None, last),
        grid=(total_rows // chunk, count),
        in_specs=in_specs,
        out_specs=row_block,
        out_shape=jax.ShapeDtypeStruct((total_rows, D), kind),
        scratch_shapes=[pltpu.VMEM((chunk, D), jnp.float32)],
        compiler_params=params("arbitrary", "arbitrary"),
        cost_estimate=pl.CostEstimate(
            flops=6 * total_rows * count * D * FF_EXPERT,
            bytes_accessed=2 * (gate_up.size + down.size) * (total_rows // chunk)
            + 8 * total_rows * D,
            transcendentals=total_rows * count * FF_EXPERT,
        ),
    )(*operands)


def shards(
    hidden_states,
    first_gain,
    second_gain,
    w_query,
    w_keyval,
    w_out,
    kv_cache,
    page_table,
    cached_len,
    expert_ids,
    gate_weights,
    w_gate_up,
    w_down,
):
    rows = hidden_states.shape[0]
    tp_size = lax.axis_size("tp")
    tp_rank = lax.axis_index("tp")
    per_request = tp_size // REQ_DEV
    request = tp_rank // per_request
    first_row = (tp_rank % per_request) * rows
    bf16 = jnp.bfloat16

    query_full = lax.all_gather(w_query, "tp", axis=1, tiled=True)
    out_full = lax.all_gather(w_out, "tp", axis=0, tiled=True)
    local = EXPERTS // tp_size
    step = max(local // EXPERT_GROUPS, 1)
    gathered = [
        (
            lax.all_gather(w_gate_up[at : at + step], "tok", axis=0),
            lax.all_gather(w_down[at : at + step], "tok", axis=0),
        )
        for at in range(0, local, step)
    ]

    expert_range = jnp.arange(EXPERTS, dtype=jnp.int32)
    dense = jnp.sum(
        jnp.where(
            expert_ids[:, :, None] == expert_range[None, None, :], gate_weights[:, :, None], 0.0
        ),
        axis=1,
    )
    dense = lax.all_gather(dense, "tp", axis=0, tiled=True)
    gates = lax.dynamic_slice_in_dim(dense, tp_rank * local, local, 1)

    length = jnp.sum(jnp.where(jnp.arange(REQ_DEV) == request, cached_len, 0))
    pages = jnp.sum(
        jnp.where(jnp.arange(REQ_DEV)[:, None] == request, page_table, 0), axis=0
    ) - lax.axis_index("tok") * kv_cache.shape[0]
    positions = (length + first_row + jnp.arange(rows, dtype=jnp.int32)).astype(jnp.float32)
    half = HEAD_DIM // 2
    frequency = jnp.power(THETA, -(jnp.arange(half).astype(jnp.float32) * (2.0 / HEAD_DIM)))
    angles = positions[:, None] * frequency[None, :]
    cosine, sine = jnp.cos(angles), jnp.sin(angles)
    cosine = jnp.concatenate([cosine] * 4, axis=1)
    sine = jnp.concatenate([-sine, sine, -sine, sine], axis=1)

    normed, keyval = pl.pallas_call(
        keyval_kernel,
        out_shape=(jax.ShapeDtypeStruct((rows, D), bf16), jax.ShapeDtypeStruct((rows, D), bf16)),
        compiler_params=params(),
        cost_estimate=pl.CostEstimate(
            flops=2 * rows * D * D, bytes_accessed=2 * D * D + 6 * rows * D, transcendentals=0
        ),
    )(hidden_states, first_gain.reshape(1, D), w_keyval, cosine, sine)
    groups = [
        [r * per_request + i for i in range(per_request)] for r in range(REQ_DEV)
    ]
    new_kv = lax.all_gather(keyval, "tp", axis=0, tiled=True, axis_index_groups=groups)
    queries = pl.pallas_call(
        query_kernel,
        out_shape=jax.ShapeDtypeStruct((rows, D), bf16),
        compiler_params=params(),
        cost_estimate=pl.CostEstimate(
            flops=2 * rows * D * D, bytes_accessed=2 * D * D + 4 * rows * D, transcendentals=0
        ),
    )(normed, query_full, cosine, sine)

    pool = kv_cache.shape[0]
    attended = pl.pallas_call(
        attention_kernel,
        grid_spec=pltpu.PrefetchScalarGridSpec(
            num_scalar_prefetch=2,
            grid=(PAIRS,),
            in_specs=[
                pl.BlockSpec((rows, 2 * LANES), lambda p, *_: (0, p)),
                pl.BlockSpec((pool, PAGE, LANES), lambda p, *_: (0, 0, p)),
                pl.BlockSpec((pool, PAGE, LANES), lambda p, *_: (0, 0, PAIRS + p)),
                pl.BlockSpec((NEW, LANES), lambda p, *_: (0, p)),
                pl.BlockSpec((NEW, LANES), lambda p, *_: (0, PAIRS + p)),
            ],
            out_specs=pl.BlockSpec((rows, 2 * LANES), lambda p, *_: (0, p)),
            scratch_shapes=[
                pltpu.VMEM((4, rows, LANES), bf16),
                pltpu.VMEM((4, rows, 1), jnp.float32),
                pltpu.VMEM((4, rows, 2 * LANES), jnp.float32),
            ],
        ),
        out_shape=jax.ShapeDtypeStruct((rows, D), bf16),
        compiler_params=params("arbitrary"),
        cost_estimate=pl.CostEstimate(
            flops=16 * rows * 3072 * D, bytes_accessed=12 * 1024 * 1024, transcendentals=rows * 3072 * 16
        ),
    )(pages, jnp.stack([length, first_row]).astype(jnp.int32), queries, kv_cache, kv_cache, new_kv, new_kv)

    middle, normed_two = pl.pallas_call(
        out_kernel,
        out_shape=(jax.ShapeDtypeStruct((rows, D), bf16), jax.ShapeDtypeStruct((rows, D), bf16)),
        compiler_params=params(),
        cost_estimate=pl.CostEstimate(
            flops=2 * rows * D * D, bytes_accessed=2 * D * D + 8 * rows * D, transcendentals=0
        ),
    )(attended, out_full, hidden_states, second_gain.reshape(1, D))

    rows_in = lax.all_gather(normed_two, "tp", axis=0, tiled=True)
    total = None
    for index, (gate_up, down) in enumerate(gathered):
        last = index == len(gathered) - 1
        part = gates[:, index * step : (index + 1) * step]
        total = experts(rows_in, part, gate_up, down, total, last)
    returned = lax.all_to_all(
        total.reshape(tp_size, rows, D), "tp", split_axis=0, concat_axis=0, tiled=True
    )
    mixture = jnp.sum(returned.astype(jnp.float32), axis=0)
    return (middle.astype(jnp.float32) + mixture).astype(bf16)


def solution(mesh):
    in_specs = (
        P(("tok", "tp"), None),
        P(),
        P(),
        P(None, "tp"),
        P(),
        P("tp", None),
        P("tok", None, None),
        P("tok", None),
        P("tok"),
        P(("tok", "tp"), None),
        P(("tok", "tp"), None),
        P("tp", "tok", None),
        P("tp", "tok", None),
    )
    out_specs = P(("tok", "tp"), None)
    return jax.shard_map(shards, mesh=mesh, in_specs=in_specs, out_specs=out_specs, check_vma=False)
```

time: 862 us -> 542 us (0.63)
  waiting for transfers between devices: 497 us -> 274 us
  matrix products: 172 us -> 0 us
  Pallas kernels: 0 us -> 163 us
  local copies, waits for them, and re-layouts: 120 us -> 5.04 us
  blocking collectives: 0 us -> 76 us
  other arithmetic: 27.9 us -> 7.93 us
  starting transfers between devices: 14.4 us -> 0.47 us
    all_to_all x2 -> x0, waiting for transfers between devices: 363 us -> none  [the longest x1 182 us: shards(): lax.all_to_all(send_buffer.reshape(tp_size, experts_local, capacity, D),...]
    all_gather x3 -> x8, waiting for transfers between devices: 48.8 us -> 272 us  [the longest x2 166 us: shards(): lax.all_gather(w_gate_up[at:at + step], 'tok', axis=0)]
    pallas_call x0 -> x6, Pallas kernels: none -> 163 us  [the longest x2 90.1 us: experts(): pl.pallas_call(functools.partial(expert_kernel, before is None, last), gr...]
    dot_general x11 -> x0, matrix products: 118 us -> none  [the longest x4 42.2 us: one_block(): jnp.einsum('gpqk,kgd->qgpd', probs, values_total, preferred_element_type=...]
    reduce_scatter x1 -> x0, waiting for transfers between devices: 83.8 us -> none  [shards(): lax.psum_scatter(jnp.dot(attended, w_out, preferred_element_type=jnp.floa...]
    sub x4 -> x0, matrix products: 54.5 us -> none  [one_block(): weights = jnp.exp(scores - top_score)]
    all_to_all x0 -> x1, blocking collectives: none -> 52.3 us  [shards(): lax.all_to_all(total.reshape(tp_size, rows, D), 'tp', split_axis=0, conca...]
    gather x5 -> x0, local copies, waits for them, and re-layouts: 36.1 us -> none  [the longest x1 29 us: shards(): picked = returned[target]]
  transfers between devices with their start and end apart: 6 -> 8, of which waited for: 4 -> 6; matrix products, arithmetic and copies ran while one was open for 10% -> 2% of each run, Pallas kernels for 0% -> 22%
where the time goes in v1:
time: 542 us; the launch traced here: 541 us
  waiting for transfers between devices  274 us (51%)
  Pallas kernels  163 us (30%)
  blocking collectives  76 us (14%)
  between operations  14.3 us (3%)
  other arithmetic  7.93 us (1%)
    all_gather x2, waiting for transfers between devices, shards(): lax.all_gather(w_gate_up[at:at + step], 'tok', axis=0)  166 us
    pallas_call x2, Pallas kernels, experts(): pl.pallas_call(functools.partial(expert_kernel, before is None, last), gr...  90.1 us
    pallas_call x1, Pallas kernels, shards(): pl.pallas_call(attention_kernel, grid_spec=pltpu.PrefetchScalarGridSpec(n...  58.8 us
    all_to_all x1, blocking collectives, shards(): lax.all_to_all(total.reshape(tp_size, rows, D), 'tp', split_axis=0, conca...  52.3 us
    all_gather x1, waiting for transfers between devices, shards(): rows_in = lax.all_gather(normed_two, 'tp', axis=0, tiled=True)  46.1 us
    all_gather x1, waiting for transfers between devices, shards(): lax.all_gather(keyval, 'tp', axis=0, tiled=True, axis_index_groups=groups)  29.9 us
    all_gather x1, waiting for transfers between devices, shards(): query_full = lax.all_gather(w_query, 'tp', axis=1, tiled=True)  26.9 us
    all_gather x1, blocking collectives, shards(): dense = lax.all_gather(dense, 'tp', axis=0, tiled=True)  23.6 us
  transfers between devices with their start and end apart: 8, of which 6 were waited for; matrix products, arithmetic and copies ran while one was open for 2% of the time, Pallas kernels for 22%

profile of v1, /device:TPU:0, one launch (start us, length us, event | category | flops | bytes accessed | tf_op | source)
XLA Modules:
  0.0 541.3 jit_solution(94521785924569640)
XLA Ops:
  6.5 0.0 copy-start.1
  6.5 0.0 all-gather.13.cloned.1.call-start
  6.5 0.7 all-gather.13.cloned.1.call-update
  7.3 0.0 all-gather.15.cloned.1.call-start
  7.3 1.4 select_reduce_fusion.2
  9.3 1.0 fusion
  10.3 1.3 pad_maximum_fusion
  11.7 0.0 copy-start.5
  11.7 4.4 shard_map.127
  16.1 0.0 all-gather.15.cloned.1.call-update
  16.2 0.0 all-gather.17.cloned.1.call-start
  16.2 0.7 all-gather.17.cloned.1.call-update
  16.9 0.0 all-gather.27.cloned.1.call-start
  16.9 0.0 copy-done.1
  17.0 1.1 fusion.2
  18.0 0.0 all-gather.27.cloned.1.call-update
  18.1 0.2 all-gather.19.cloned.1.call-start
  18.3 1.2 pad_add_fusion.sizes_ref
  19.5 0.0 copy-done.5
  19.5 0.1 select_reduce_fusion.1
  19.6 0.6 broadcast_subtract_fusion.pages_ref
  20.2 26.9 %all-gather.13.cloned.1.call-done.w_ref = bf16[1024,1024]{1,0:T(8,128)(2,1)} async-done(((bf16[1024,256]{1,0:T(8,128)(2,1)}), bf16[1024,1024]{1,0:T(8,128)(2,1)}) %all-gather.13.cloned.1.call-update) | async-done | bytes 2097168 | tf_op jit(solution)/shard_map/all_gather | solution.py:254
  47.1 4.8 shard_map.128.q_ref
  51.9 29.9 %all-gather.15.cloned.1.call-done.nk_ref.nv_ref = bf16[1024,1024]{1,0:T(8,128)(2,1)} async-done(((bf16[512,1024]{1,0:T(8,128)(2,1)}), bf16[1024,1024]{1,0:T(8,128)(2,1)}) %all-gather.15.cloned.1.call-update) | async-done | bytes 2097168 | tf_op jit(solution)/shard_map/all_gather | solution.py:299
  81.8 58.8 %shard_map.129.att_ref = bf16[512,1024]{1,0:T(8,128)(2,1)} custom-call(s32[16]{0:T(128)} %broadcast_subtract_fusion.pages_ref, s32[2]{0:T(128)} %pad_add_fusion.sizes_ref, bf16[512,1024]{1,0:T(8,128)(2,1)} %shard_map.128.q_ref, bf16[24,128,1024]{2,1,0:T(8,128)(2,1)} %cv_ref.1, bf16[24,128,1024]{2,1,0:T(8,128)(2,1)} %cv_ref.1, ...), custom_call_target="tpu_custom_call" | custom-call | flops 25769803776 | bytes 12582912 | tf_op jit(solution)/shard_map/pallas_call | solution.py:310
  140.6 0.0 copy-start
  140.6 0.0 all-gather.17.cloned.1.call-done.w_ref
  140.6 5.1 shard_map.130
  145.7 0.0 copy-start.3
  145.7 0.0 copy-start.4
  145.7 0.0 all-gather.19.cloned.1.call-update
  145.7 0.0 all-gather.25.cloned.1.call-start
  145.7 0.0 copy-done
  145.8 1.6 fusion.1
  147.4 0.0 all-gather.25.cloned.1.call-update
  147.4 0.0 all-gather.23.cloned.1.call-start
  147.4 0.7 all-gather.23.cloned.1.call-update
  148.1 0.0 all-gather.21.cloned.1.call-start
  148.2 0.7 all-gather.21.cloned.1.call-update
  148.9 0.0 copy-done.3
  148.9 0.0 copy-done.4
  148.9 0.1 select_reduce_fusion
  149.0 0.1 copy.20
  149.1 23.6 %all_gather.43 = f32[2048,32]{1,0:T(8,128)S(1)} all-gather(f32[512,32]{1,0:T(8,128)S(1)} %copy.20), channel_id=1, replica_groups=mesh['tok'=8,'tp'=4] {'tp'}, dimensions={0}, use_global_device_ids=true | all-gather | bytes 327680 | tf_op jit(solution)/shard_map/all_gather | solution.py:273
  172.8 1.9 constant_dynamic-slice_fusion.1
  174.7 0.0 all-gather.27.cloned.1.call-done
  174.7 46.1 %all-gather.19.cloned.1.call-done.x_ref = bf16[2048,1024]{1,0:T(8,128)(2,1)} async-done(((bf16[512,1024]{1,0:T(8,128)(2,1)}), bf16[2048,1024]{1,0:T(8,128)(2,1)}) %all-gather.19.cloned.1.call-update) | async-done | bytes 4194320 | tf_op jit(solution)/shard_map/all_gather | solution.py:345
  220.8 83.5 %all-gather.25.cloned.1.call-done = bf16[32,128,1024]{2,1,0:T(8,128)(2,1)} async-done(((bf16[4,128,1024]{2,1,0:T(8,128)(2,1)}), bf16[32,128,1024]{2,1,0:T(8,128)(2,1)}) %all-gather.25.cloned.1.call-update) | async-done | bytes 8388624 | tf_op jit(solution)/shard_map/all_gather | solution.py:260
  304.3 44.5 %shard_map.131.rest_0_ = f32[2048,1024]{1,0:T(8,128)} custom-call(bf16[2048,1024]{1,0:T(8,128)(2,1)} %all-gather.19.cloned.1.call-done.x_ref, f32[2048,4]{1,0:T(8,128)} %get-tuple-element.17.gates_ref, bf16[8,4,128,1024]{3,2,1,0:T(8,128)(2,1)} %bitcast.11, bf16[8,4,64,1024]{3,2,1,0:T(8,128)(2,1)} %bitcast.13), custom_call_target="tpu_custom_call" | custom-call | flops 25769803776 | bytes 41943040 | tf_op jit(solution)/shard_map/pallas_call | solution.py:214
  348.8 2.9 all-gather.23.cloned.1.call-done
  351.7 82.4 %all-gather.21.cloned.1.call-done = bf16[32,128,1024]{2,1,0:T(8,128)(2,1)} async-done(((bf16[4,128,1024]{2,1,0:T(8,128)(2,1)}), bf16[32,128,1024]{2,1,0:T(8,128)(2,1)}) %all-gather.21.cloned.1.call-update) | async-done | bytes 8388624 | tf_op jit(solution)/shard_map/all_gather | solution.py:260
  434.0 45.6 %shard_map.132 = bf16[2048,1024]{1,0:T(8,128)(2,1)} custom-call(bf16[2048,1024]{1,0:T(8,128)(2,1)} %all-gather.19.cloned.1.call-done.x_ref, f32[2048,4]{1,0:T(8,128)} %get-tuple-element.18.gates_ref, bf16[8,4,128,1024]{3,2,1,0:T(8,128)(2,1)} %bitcast.12, bf16[8,4,64,1024]{3,2,1,0:T(8,128)(2,1)} %bitcast.14, f32[2048,1024]{1,0:T(8,128)} %shard_map.131.rest_0_), custom_call_target="tpu_custom_call" | custom-call | flops 25769803776 | bytes 41943040 | tf_op jit(solution)/shard_map/pallas_call | solution.py:214
  479.6 52.3 %all_to_all.5 = bf16[4,512,1024]{2,1,0:T(8,128)(2,1)S(1)} all-to-all(bf16[4,512,1024]{2,1,0:T(8,128)(2,1)} %bitcast.9), channel_id=1, replica_groups=mesh['tok'=8,'tp'=4] {'tp'}, dimensions={0} | all-to-all | bytes 8388608 | tf_op jit(solution)/shard_map/all_to_all | solution.py:351
  531.9 0.0 copy-start.2
  531.9 0.9 convert_reduce_fusion
  532.9 0.3 copy-done.2
  533.1 1.3 add_convert_fusion
  (3 shorter events, 0.0 us)
Async XLA Ops:
  6.5 10.4 %copy-start.1 = (bf16[8,64,1024]{2,1,0:T(8,128)(2,1)S(1)}, bf16[8,64,1024]{2,1,0:T(8,128)(2,1)}, u32[]{:S(2)}) copy-start(bf16[8,64,1024]{2,1,0:T(8,128)(2,1)} %param.25) | copy-start | bytes 3145732
  6.5 40.5 %all-gather.13.cloned.1.call-start = ((), (), s32[]{:S(2)}) async-start(), calls=%async_computation.1 | async-start | bytes 2621440 | tf_op jit(solution)/shard_map/all_gather | solution.py:254
  7.3 74.5 %all-gather.15.cloned.1.call-start = ((), (), s32[]{:S(2)}) async-start(), calls=%async_computation.2 | async-start | bytes 3145728 | tf_op jit(solution)/shard_map/all_gather | solution.py:299
  11.7 7.9 %copy-start.5 = (s32[2,16]{1,0:T(2,128)S(1)}, s32[2,16]{1,0:T(2,128)}, u32[]{:S(2)}) copy-start(s32[2,16]{1,0:T(2,128)} %param.20) | copy-start | bytes 388
  16.2 124.4 %all-gather.17.cloned.1.call-start = ((), (), s32[]{:S(2)}) async-start(), calls=%async_computation.3 | async-start | bytes 2621440 | tf_op jit(solution)/shard_map/all_gather | solution.py:255
  16.9 157.8 %all-gather.27.cloned.1.call-start = ((), (), s32[]{:S(2)}) async-start(), calls=%async_computation.8 | async-start | bytes 4718592 | tf_op jit(solution)/shard_map/all_gather | solution.py:261
  18.1 202.7 %all-gather.19.cloned.1.call-start = ((), (), s32[]{:S(2)}) async-start(), calls=%async_computation.4 | async-start | bytes 5242880 | tf_op jit(solution)/shard_map/all_gather | solution.py:345
  140.6 5.2 copy-start
  145.7 3.2 copy-start.3
  145.7 3.2 copy-start.4
  145.7 158.6 %all-gather.25.cloned.1.call-start = ((), (), s32[]{:S(2)}) async-start(), calls=%async_computation.7 | async-start | bytes 9437184 | tf_op jit(solution)/shard_map/all_gather | solution.py:260
  147.4 204.3 %all-gather.23.cloned.1.call-start = ((), (), s32[]{:S(2)}) async-start(), calls=%async_computation.6 | async-start | bytes 4718592 | tf_op jit(solution)/shard_map/all_gather | solution.py:261
  148.1 285.9 %all-gather.21.cloned.1.call-start = ((), (), s32[]{:S(2)}) async-start(), calls=%async_computation.5 | async-start | bytes 9437184 | tf_op jit(solution)/shard_map/all_gather | solution.py:260
  531.9 1.2 copy-start.2
Sparse Core Ops, SparseCore 0:
  9.2 37.8 all-gather.12
  48.6 33.1 all-gather.14
  83.6 35.3 all-gather.16
  120.4 47.1 all-gather.26
  169.3 51.4 all-gather.18
  222.2 82.0 all-gather.24
  305.9 45.7 all-gather.22
  353.3 80.7 all-gather.20

commit v2 on v1

--- a/solution.py
+++ b/solution.py
@@ -26,7 +26,7 @@
 LANES = 128
 PAIRS = KV_HEADS // 2
 KEY_BLOCK = 512
-EXPERT_GROUPS = 2
+EXPERT_GROUPS = 4
 NEGATIVE = -1e30
 VMEM_LIMIT = 56 * 1024 * 1024
 
@@ -228,6 +228,23 @@
     )(*operands)
 
 
+def exchange(block, shift, size):
+    return lax.ppermute(block, "tp", [(i, i ^ shift) for i in range(size)])
+
+
+def collect(block, axis, count, size):
+    width = block.shape[axis]
+    place = lax.axis_index("tp") % count
+    shape = list(block.shape)
+    shape[axis] = width * count
+    whole = jnp.zeros(shape, block.dtype)
+    for shift in range(count):
+        piece = block if shift == 0 else exchange(block, shift, size)
+        owner = jnp.bitwise_xor(place, shift)
+        whole = lax.dynamic_update_slice_in_dim(whole, piece, owner * width, axis)
+    return whole
+
+
 def shards(
     hidden_states,
     first_gain,
@@ -251,8 +268,8 @@
     first_row = (tp_rank % per_request) * rows
     bf16 = jnp.bfloat16
 
-    query_full = lax.all_gather(w_query, "tp", axis=1, tiled=True)
-    out_full = lax.all_gather(w_out, "tp", axis=0, tiled=True)
+    query_full = collect(w_query, 1, tp_size, tp_size)
+    out_full = collect(w_out, 0, tp_size, tp_size)
     local = EXPERTS // tp_size
     step = max(local // EXPERT_GROUPS, 1)
     gathered = [
@@ -270,8 +287,12 @@
         ),
         axis=1,
     )
-    dense = lax.all_gather(dense, "tp", axis=0, tiled=True)
-    gates = lax.dynamic_slice_in_dim(dense, tp_rank * local, local, 1)
+    gates = [
+        lax.dynamic_slice_in_dim(
+            exchange(dense, shift, tp_size) if shift else dense, tp_rank * local, local, 1
+        )
+        for shift in range(tp_size)
+    ]
 
     length = jnp.sum(jnp.where(jnp.arange(REQ_DEV) == request, cached_len, 0))
     pages = jnp.sum(
@@ -293,10 +314,7 @@
             flops=2 * rows * D * D, bytes_accessed=2 * D * D + 6 * rows * D, transcendentals=0
         ),
     )(hidden_states, first_gain.reshape(1, D), w_keyval, cosine, sine)
-    groups = [
-        [r * per_request + i for i in range(per_request)] for r in range(REQ_DEV)
-    ]
-    new_kv = lax.all_gather(keyval, "tp", axis=0, tiled=True, axis_index_groups=groups)
+    new_kv = collect(keyval, 0, per_request, tp_size)
     queries = pl.pallas_call(
         query_kernel,
         out_shape=jax.ShapeDtypeStruct((rows, D), bf16),
@@ -342,16 +360,23 @@
         ),
     )(attended, out_full, hidden_states, second_gain.reshape(1, D))
 
-    rows_in = lax.all_gather(normed_two, "tp", axis=0, tiled=True)
-    total = None
+    shifts = list(range(tp_size))
+    rows_in = [exchange(normed_two, shift, tp_size) if shift else normed_two for shift in shifts]
+    totals = [None] * tp_size
+    returned = [None] * tp_size
     for index, (gate_up, down) in enumerate(gathered):
         last = index == len(gathered) - 1
-        part = gates[:, index * step : (index + 1) * step]
-        total = experts(rows_in, part, gate_up, down, total, last)
-    returned = lax.all_to_all(
-        total.reshape(tp_size, rows, D), "tp", split_axis=0, concat_axis=0, tiled=True
-    )
-    mixture = jnp.sum(returned.astype(jnp.float32), axis=0)
+        span = slice(index * step, (index + 1) * step)
+        for shift in reversed(shifts) if last else shifts:
+            totals[shift] = experts(
+                rows_in[shift], gates[shift][:, span], gate_up, down, totals[shift], last
+            )
+            if last:
+                made = totals[shift]
+                returned[shift] = exchange(made, shift, tp_size) if shift else made
+        if not last:
+            totals = list(lax.optimization_barrier(tuple(totals)))
+    mixture = sum(part.astype(jnp.float32) for part in returned)
     return (middle.astype(jnp.float32) + mixture).astype(bf16)
 
 

time: 542 us -> 406 us (0.75)
  waiting for transfers between devices: 274 us -> 84.5 us
  blocking collectives: 76 us -> 0 us
  starting transfers between devices: 0.47 us -> 67.2 us
  Pallas kernels: 163 us -> 202 us
  local copies, waits for them, and re-layouts: 5.04 us -> 23.4 us
    all_gather x2 -> x4, waiting for transfers between devices: 166 us -> 2.33 us  [shards(): lax.all_gather(w_gate_up[at:at + step], 'tok', axis=0)]
    all_gather x4 -> x0, waiting for transfers between devices: 103 us -> none  [the longest x1 46.1 us: shards(): rows_in = lax.all_gather(normed_two, 'tp', axis=0, tiled=True)]
    ppermute x0 -> x16, waiting for transfers between devices: none -> 79.1 us  [exchange(): return lax.ppermute(block, 'tp', [(i, i ^ shift) for i in range(size)])]
    ppermute x0 -> x16, starting transfers between devices: none -> 66.9 us  [exchange(): return lax.ppermute(block, 'tp', [(i, i ^ shift) for i in range(size)])]
    pallas_call x2 -> x16, Pallas kernels: 90.1 us -> 150 us  [experts(): pl.pallas_call(functools.partial(expert_kernel, before is None, last), gr...]
    all_to_all x1 -> x0, blocking collectives: 52.3 us -> none  [shards(): lax.all_to_all(total.reshape(tp_size, rows, D), 'tp', split_axis=0, conca...]
    all_gather x1 -> x0, blocking collectives: 23.6 us -> none  [shards(): dense = lax.all_gather(dense, 'tp', axis=0, tiled=True)]
    pallas_call x1, Pallas kernels: 58.8 us -> 37.7 us  [shards(): pl.pallas_call(attention_kernel, grid_spec=pltpu.PrefetchScalarGridSpec(n...]
  transfers between devices with their start and end apart: 8 -> 24, of which waited for: 6 -> 5; matrix products, arithmetic and copies ran while one was open for 2% -> 6% of each run, Pallas kernels for 22% -> 48%
where the time goes in v2:
time: 406 us; the launch traced here: 400 us
  Pallas kernels  202 us (50%)
  waiting for transfers between devices  84.5 us (21%)
  starting transfers between devices  67.2 us (17%)
  local copies, waits for them, and re-layouts  23.4 us (6%)
  between operations  14.9 us (4%)
  other arithmetic  8.38 us (2%)
    pallas_call x16, Pallas kernels, experts(): pl.pallas_call(functools.partial(expert_kernel, before is None, last), gr...  150 us
    ppermute x16, waiting for transfers between devices, exchange(): return lax.ppermute(block, 'tp', [(i, i ^ shift) for i in range(size)])  79.1 us
    ppermute x16, starting transfers between devices, exchange(): return lax.ppermute(block, 'tp', [(i, i ^ shift) for i in range(size)])  66.9 us
    pallas_call x1, Pallas kernels, shards(): pl.pallas_call(attention_kernel, grid_spec=pltpu.PrefetchScalarGridSpec(n...  37.7 us
    dynamic_update_slice x10, local copies, waits for them, and re-layouts, collect(): whole = lax.dynamic_update_slice_in_dim(whole, piece, owner * width, axis)  9.71 us
  transfers between devices with their start and end apart: 24, of which 5 were waited for; matrix products, arithmetic and copies ran while one was open for 6% of the time, Pallas kernels for 48%

profile of v2, /device:TPU:0, one launch (start us, length us, event | category | flops | bytes accessed | tf_op | source)
XLA Modules:
  0.0 400.2 jit_solution(9301151371265017468)
XLA Ops:
  6.5 2.4 fusion.2
  9.0 1.3 fusion.1
  10.4 0.7 all-gather.27.cloned.1.call-update
  11.1 0.5 all-gather.25.cloned.1.call-update
  11.7 0.5 all-gather.23.cloned.1.call-update
  12.9 0.7 all-gather.19.cloned.1.call-update
  13.6 3.0 collective-permute-start
  16.6 1.5 collective-permute-start.1
  18.2 0.7 select_reduce_fusion.2
  19.6 1.0 fusion
  20.6 1.3 pad_maximum_fusion
  21.9 4.4 %shard_map.127 = (bf16[512,1024]{1,0:T(8,128)(2,1)}, bf16[512,1024]{1,0:T(8,128)(2,1)}) custom-call(bf16[512,1024]{1,0:T(8,128)(2,1)} %x_ref.3, f32[1,1024]{1,0:T(1,128)} %bitcast.45, bf16[1024,1024]{1,0:T(8,128)(2,1)} %w_ref.1, f32[512,128]{1,0:T(8,128)} %get-tuple-element.64.cos_ref, f32[512,128]{1,0:T(8,128)} %get-tuple-element.65.sin_ref), custom_call_target="tpu_custom_call" | custom-call | flops 1073741824 | bytes 5242880 | tf_op jit(solution)/shard_map/pallas_call | solution.py:309
  26.3 2.0 collective-permute-start.3
  28.5 0.5 broadcast_subtract_fusion.pages_ref
  29.3 1.1 constant_dynamic-update-slice_fusion.9
  30.7 1.5 constant_dynamic-update-slice_fusion.3
  32.2 1.3 pad_add_fusion.sizes_ref
  33.8 1.5 constant_dynamic-update-slice_fusion.5
  35.3 2.0 collective-permute-start.5
  37.3 1.1 constant_dynamic-update-slice_fusion.8
  38.4 35.4 %collective-permute-done.4 = bf16[256,1024]{1,0:T(8,128)(2,1)} collective-permute-done((bf16[256,1024]{1,0:T(8,128)(2,1)}, bf16[256,1024]{1,0:T(8,128)(2,1)}, u32[]{:S(2)}, u32[]{:S(2)}) %collective-permute-start.4) | collective-permute-done | bytes 524320 | tf_op jit(solution)/shard_map/ppermute | solution.py:232
  73.8 2.7 collective-permute-start.6
  76.5 1.1 constant_dynamic-update-slice_fusion.2
  77.6 1.1 constant_dynamic-update-slice_fusion.7
  78.8 1.1 constant_dynamic-update-slice_fusion.6.w_ref
  79.9 1.3 copy-done.3
  81.2 4.7 %shard_map.128.q_ref = bf16[512,1024]{1,0:T(8,128)(2,1)} custom-call(bf16[512,1024]{1,0:T(8,128)(2,1)} %get-tuple-element.21.normed_ref, bf16[1024,1024]{1,0:T(8,128)(2,1)} %copy-done.3, f32[512,128]{1,0:T(8,128)} %get-tuple-element.64.cos_ref, f32[512,128]{1,0:T(8,128)} %get-tuple-element.65.sin_ref), custom_call_target="tpu_custom_call" | custom-call | flops 1073741824 | bytes 4194304 | tf_op jit(solution)/shard_map/pallas_call | solution.py:318
  85.9 2.2 collective-permute-done.6
  88.2 1.1 constant_dynamic-update-slice_fusion.w_ref
  89.4 1.5 copy-done.4
  90.9 37.7 %shard_map.129.att_ref = bf16[512,1024]{1,0:T(8,128)(2,1)} custom-call(s32[16]{0:T(128)} %broadcast_subtract_fusion.pages_ref, s32[2]{0:T(128)} %pad_add_fusion.sizes_ref, bf16[512,1024]{1,0:T(8,128)(2,1)} %shard_map.128.q_ref, bf16[24,128,1024]{2,1,0:T(8,128)(2,1)} %cv_ref.1, bf16[24,128,1024]{2,1,0:T(8,128)(2,1)} %cv_ref.1, bf16[1024,1024]{1,0:T(8,128)(2,1)} %copy-done.4, ...), custom_call_target="tpu_custom_call" | custom-call | flops 25769803776 | bytes 12582912 | tf_op jit(solution)/shard_map/pallas_call | solution.py:328
  128.7 4.8 %shard_map.130 = (bf16[512,1024]{1,0:T(8,128)(2,1)}, bf16[512,1024]{1,0:T(8,128)(2,1)}) custom-call(bf16[512,1024]{1,0:T(8,128)(2,1)} %shard_map.129.att_ref, bf16[1024,1024]{1,0:T(8,128)(2,1)} %copy-done, bf16[512,1024]{1,0:T(8,128)(2,1)} %x_ref.3, f32[1,1024]{1,0:T(1,128)} %bitcast.12), custom_call_target="tpu_custom_call" | custom-call | flops 1073741824 | bytes 6291456 | tf_op jit(solution)/shard_map/pallas_call | solution.py:354
  133.5 12.3 %collective-permute-start.7 = (bf16[512,1024]{1,0:T(8,128)(2,1)}, bf16[512,1024]{1,0:T(8,128)(2,1)S(1)}, u32[]{:S(2)}, u32[]{:S(2)}) collective-permute-start(bf16[512,1024]{1,0:T(8,128)(2,1)} %get-tuple-element.24.x_ref), channel_id=1, source_target_pairs={{0,1},{1,0},{2,3},{3,2},{4,5},{5,4},{6,7},{7,6},{8,9},{9,8},{10,11... | collective-permute-start | bytes 3145736 | tf_op jit(solution)/shard_map/ppermute | solution.py:232
  146.0 22.8 %collective-permute-start.10 = (f32[512,32]{1,0:T(8,128)S(1)}, f32[512,32]{1,0:T(8,128)S(1)}, u32[]{:S(2)}, u32[]{:S(2)}) collective-permute-start(f32[512,32]{1,0:T(8,128)S(1)} %copy.23), channel_id=1, source_target_pairs={{0,2},{1,3},{2,0},{3,1},{4,6},{5,7},{6,4},{7,5},{8,10},{9,11},{10,... | collective-permute-start | bytes 196616 | tf_op jit(solution)/shard_map/ppermute | solution.py:232
  168.8 1.4 collective-permute-start.12
  170.2 2.0 collective-permute-start.9
  172.2 1.3 constant_dynamic-slice_fusion.11
  173.5 1.3 constant_dynamic-slice_fusion.14
  174.8 13.6 %collective-permute-start.11 = (bf16[512,1024]{1,0:T(8,128)(2,1)S(1)}, bf16[512,1024]{1,0:T(8,128)(2,1)}, u32[]{:S(2)}, u32[]{:S(2)}) collective-permute-start(bf16[512,1024]{1,0:T(8,128)(2,1)S(1)} %copy-done.10), channel_id=1, source_target_pairs={{0,3},{1,2},{2,1},{3,0},{4,7},{5,6},{6,5},{7,4},{8,11},{9,10},{10,... | collective-permute-start | bytes 3145736 | tf_op jit(solution)/shard_map/ppermute | solution.py:232
  188.4 1.4 constant_dynamic-slice_fusion.13
  189.8 1.3 constant_dynamic-slice_fusion
  191.1 8.9 %shard_map.131.rest_0_ = f32[512,1024]{1,0:T(8,128)} custom-call(bf16[512,1024]{1,0:T(8,128)(2,1)} %get-tuple-element.24.x_ref, f32[512,2]{1,0:T(8,128)} %get-tuple-element.48.gates_ref, bf16[8,2,128,1024]{3,2,1,0:T(8,128)(2,1)} %bitcast.21, bf16[8,2,64,1024]{3,2,1,0:T(8,128)(2,1)} %bitcast.33), custom_call_target="tpu_custom_call" | custom-call | flops 3221225472 | bytes 10485760 | tf_op jit(solution)/shard_map/pallas_call | solution.py:214
  200.1 1.0 copy-done.11
  201.0 8.7 %shard_map.132.rest_0_ = f32[512,1024]{1,0:T(8,128)} custom-call(bf16[512,1024]{1,0:T(8,128)(2,1)} %copy-done.11, f32[512,2]{1,0:T(8,128)} %get-tuple-element.52.gates_ref, bf16[8,2,128,1024]{3,2,1,0:T(8,128)(2,1)} %bitcast.22, bf16[8,2,64,1024]{3,2,1,0:T(8,128)(2,1)} %bitcast.34), custom_call_target="tpu_custom_call" | custom-call | flops 3221225472 | bytes 10485760 | tf_op jit(solution)/shard_map/pallas_call | solution.py:214
  209.7 14.2 %collective-permute-done.9.x_ref = bf16[512,1024]{1,0:T(8,128)(2,1)} collective-permute-done((bf16[512,1024]{1,0:T(8,128)(2,1)}, bf16[512,1024]{1,0:T(8,128)(2,1)}, u32[]{:S(2)}, u32[]{:S(2)}) %collective-permute-start.9) | collective-permute-done | bytes 1048608 | tf_op jit(solution)/shard_map/ppermute | solution.py:232
  223.9 8.8 %shard_map.133.rest_0_ = f32[512,1024]{1,0:T(8,128)} custom-call(bf16[512,1024]{1,0:T(8,128)(2,1)} %collective-permute-done.9.x_ref, f32[512,2]{1,0:T(8,128)} %get-tuple-element.56.gates_ref, bf16[8,2,128,1024]{3,2,1,0:T(8,128)(2,1)} %bitcast.23, bf16[8,2,64,1024]{3,2,1,0:T(8,128)(2,1)} %bitcast.35), custom_call_target="tpu_custom_call" | custom-call | flops 3221225472 | bytes 10485760 | tf_op jit(solution)/shard_map/pallas_call | solution.py:214
  232.7 8.7 %shard_map.134.rest_0_ = f32[512,1024]{1,0:T(8,128)} custom-call(bf16[512,1024]{1,0:T(8,128)(2,1)} %collective-permute-done.11.x_ref, f32[512,2]{1,0:T(8,128)} %get-tuple-element.59.gates_ref, bf16[8,2,128,1024]{3,2,1,0:T(8,128)(2,1)} %bitcast.24, bf16[8,2,64,1024]{3,2,1,0:T(8,128)(2,1)} %bitcast.36), custom_call_target="tpu_custom_call" | custom-call | flops 3221225472 | bytes 10485760 | tf_op jit(solution)/shard_map/pallas_call | solution.py:214
  241.4 9.7 %shard_map.135.rest_0_ = f32[512,1024]{1,0:T(8,128)} custom-call(bf16[512,1024]{1,0:T(8,128)(2,1)} %get-tuple-element.24.x_ref, f32[512,2]{1,0:T(8,128)} %get-tuple-element.46.gates_ref, bf16[8,2,128,1024]{3,2,1,0:T(8,128)(2,1)} %bitcast.17, bf16[8,2,64,1024]{3,2,1,0:T(8,128)(2,1)} %bitcast.41, f32[512,1024]{1,0:T(8,128)} %shard_map.131.rest_0_), custom_call_target="tpu_custom_call" | custom-call | flops 3221225472 | bytes 10485760 | tf_op jit(solution)/shard_map/pallas_call | solution.py:214
  251.1 9.8 %shard_map.138.rest_0_ = f32[512,1024]{1,0:T(8,128)} custom-call(bf16[512,1024]{1,0:T(8,128)(2,1)} %collective-permute-done.11.x_ref, f32[512,2]{1,0:T(8,128)} %get-tuple-element.58.gates_ref, bf16[8,2,128,1024]{3,2,1,0:T(8,128)(2,1)} %bitcast.18, bf16[8,2,64,1024]{3,2,1,0:T(8,128)(2,1)} %bitcast.42, f32[512,1024]{1,0:T(8,128)} %shard_map.134.rest_0_), custom_call_target="tpu_custom_call" | custom-call | flops 3221225472 | bytes 10485760 | tf_op jit(solution)/shard_map/pallas_call | solution.py:214
  260.9 9.6 %shard_map.137.rest_0_ = f32[512,1024]{1,0:T(8,128)} custom-call(bf16[512,1024]{1,0:T(8,128)(2,1)} %collective-permute-done.9.x_ref, f32[512,2]{1,0:T(8,128)} %get-tuple-element.55.gates_ref, bf16[8,2,128,1024]{3,2,1,0:T(8,128)(2,1)} %bitcast.19, bf16[8,2,64,1024]{3,2,1,0:T(8,128)(2,1)} %bitcast.43, f32[512,1024]{1,0:T(8,128)} %shard_map.133.rest_0_), custom_call_target="tpu_custom_call" | custom-call | flops 3221225472 | bytes 10485760 | tf_op jit(solution)/shard_map/pallas_call | solution.py:214
  270.6 9.7 %shard_map.136.rest_0_ = f32[512,1024]{1,0:T(8,128)} custom-call(bf16[512,1024]{1,0:T(8,128)(2,1)} %copy-done.11, f32[512,2]{1,0:T(8,128)} %get-tuple-element.51.gates_ref, bf16[8,2,128,1024]{3,2,1,0:T(8,128)(2,1)} %bitcast.20, bf16[8,2,64,1024]{3,2,1,0:T(8,128)(2,1)} %bitcast.44, f32[512,1024]{1,0:T(8,128)} %shard_map.132.rest_0_), custom_call_target="tpu_custom_call" | custom-call | flops 3221225472 | bytes 10485760 | tf_op jit(solution)/shard_map/pallas_call | solution.py:214
  280.2 10.3 %shard_map.139.rest_0_ = f32[512,1024]{1,0:T(8,128)} custom-call(bf16[512,1024]{1,0:T(8,128)(2,1)} %get-tuple-element.24.x_ref, f32[512,2]{1,0:T(8,128)} %get-tuple-element.47.gates_ref, bf16[8,2,128,1024]{3,2,1,0:T(8,128)(2,1)} %bitcast.13, bf16[8,2,64,1024]{3,2,1,0:T(8,128)(2,1)} %bitcast.37, f32[512,1024]{1,0:T(8,128)} %shard_map.135.rest_0_), custom_call_target="tpu_custom_call" | custom-call | flops 3221225472 | bytes 10485760 | tf_op jit(solution)/shard_map/pallas_call | solution.py:214
  290.6 9.7 %shard_map.142.rest_0_ = f32[512,1024]{1,0:T(8,128)} custom-call(bf16[512,1024]{1,0:T(8,128)(2,1)} %collective-permute-done.11.x_ref, f32[512,2]{1,0:T(8,128)} %get-tuple-element.57.gates_ref, bf16[8,2,128,1024]{3,2,1,0:T(8,128)(2,1)} %bitcast.14, bf16[8,2,64,1024]{3,2,1,0:T(8,128)(2,1)} %bitcast.38, f32[512,1024]{1,0:T(8,128)} %shard_map.138.rest_0_), custom_call_target="tpu_custom_call" | custom-call | flops 3221225472 | bytes 10485760 | tf_op jit(solution)/shard_map/pallas_call | solution.py:214
  300.3 9.6 %shard_map.141.rest_0_ = f32[512,1024]{1,0:T(8,128)} custom-call(bf16[512,1024]{1,0:T(8,128)(2,1)} %collective-permute-done.9.x_ref, f32[512,2]{1,0:T(8,128)} %get-tuple-element.54.gates_ref, bf16[8,2,128,1024]{3,2,1,0:T(8,128)(2,1)} %bitcast.15, bf16[8,2,64,1024]{3,2,1,0:T(8,128)(2,1)} %bitcast.39, f32[512,1024]{1,0:T(8,128)} %shard_map.137.rest_0_), custom_call_target="tpu_custom_call" | custom-call | flops 3221225472 | bytes 10485760 | tf_op jit(solution)/shard_map/pallas_call | solution.py:214
  309.9 9.6 %shard_map.140.rest_0_ = f32[512,1024]{1,0:T(8,128)} custom-call(bf16[512,1024]{1,0:T(8,128)(2,1)} %copy-done.11, f32[512,2]{1,0:T(8,128)} %get-tuple-element.50.gates_ref, bf16[8,2,128,1024]{3,2,1,0:T(8,128)(2,1)} %bitcast.16, bf16[8,2,64,1024]{3,2,1,0:T(8,128)(2,1)} %bitcast.40, f32[512,1024]{1,0:T(8,128)} %shard_map.136.rest_0_), custom_call_target="tpu_custom_call" | custom-call | flops 3221225472 | bytes 10485760 | tf_op jit(solution)/shard_map/pallas_call | solution.py:214
  319.5 2.3 all-gather.17.cloned.1.call-done
  321.9 9.2 %shard_map.144 = bf16[512,1024]{1,0:T(8,128)(2,1)} custom-call(bf16[512,1024]{1,0:T(8,128)(2,1)} %copy-done.11, f32[512,2]{1,0:T(8,128)} %get-tuple-element.49.gates_ref, bf16[8,2,128,1024]{3,2,1,0:T(8,128)(2,1)} %bitcast.25, bf16[8,2,64,1024]{3,2,1,0:T(8,128)(2,1)} %bitcast.29, f32[512,1024]{1,0:T(8,128)} %shard_map.140.rest_0_), custom_call_target="tpu_custom_call" | custom-call | flops 3221225472 | bytes 10485760 | tf_op jit(solution)/shard_map/pallas_call | solution.py:214
  331.1 1.5 collective-permute-start.13
  332.6 9.2 %shard_map.145 = bf16[512,1024]{1,0:T(8,128)(2,1)} custom-call(bf16[512,1024]{1,0:T(8,128)(2,1)} %collective-permute-done.9.x_ref, f32[512,2]{1,0:T(8,128)} %get-tuple-element.53.gates_ref, bf16[8,2,128,1024]{3,2,1,0:T(8,128)(2,1)} %bitcast.26, bf16[8,2,64,1024]{3,2,1,0:T(8,128)(2,1)} %bitcast.30, f32[512,1024]{1,0:T(8,128)} %shard_map.141.rest_0_), custom_call_target="tpu_custom_call" | custom-call | flops 3221225472 | bytes 10485760 | tf_op jit(solution)/shard_map/pallas_call | solution.py:214
  341.8 1.5 collective-permute-start.14
  343.3 9.2 %shard_map.146 = bf16[512,1024]{1,0:T(8,128)(2,1)} custom-call(bf16[512,1024]{1,0:T(8,128)(2,1)} %collective-permute-done.11.x_ref, f32[512,2]{1,0:T(8,128)} %get-tuple-element.60.gates_ref, bf16[8,2,128,1024]{3,2,1,0:T(8,128)(2,1)} %bitcast.27, bf16[8,2,64,1024]{3,2,1,0:T(8,128)(2,1)} %bitcast.31, f32[512,1024]{1,0:T(8,128)} %shard_map.142.rest_0_), custom_call_target="tpu_custom_call" | custom-call | flops 3221225472 | bytes 10485760 | tf_op jit(solution)/shard_map/pallas_call | solution.py:214
  353.0 9.3 %shard_map.143 = bf16[512,1024]{1,0:T(8,128)(2,1)} custom-call(bf16[512,1024]{1,0:T(8,128)(2,1)} %get-tuple-element.24.x_ref, f32[512,2]{1,0:T(8,128)} %get-tuple-element.45.gates_ref, bf16[8,2,128,1024]{3,2,1,0:T(8,128)(2,1)} %bitcast.28, bf16[8,2,64,1024]{3,2,1,0:T(8,128)(2,1)} %bitcast.32, f32[512,1024]{1,0:T(8,128)} %shard_map.139.rest_0_), custom_call_target="tpu_custom_call" | custom-call | flops 3221225472 | bytes 10485760 | tf_op jit(solution)/shard_map/pallas_call | solution.py:214
  362.3 27.2 %collective-permute-done.14 = bf16[512,1024]{1,0:T(8,128)(2,1)S(1)} collective-permute-done((bf16[512,1024]{1,0:T(8,128)(2,1)}, bf16[512,1024]{1,0:T(8,128)(2,1)S(1)}, u32[]{:S(2)}, u32[]{:S(2)}) %collective-permute-start.14) | collective-permute-done | bytes 1048608 | tf_op jit(solution)/shard_map/ppermute | solution.py:232
  389.5 3.4 add_convert_fusion
  (69 shorter events, 2.8 us)
Async XLA Ops:
  6.5 2.4 copy-start.5
  6.5 184.6 %all-gather.31.cloned.1.call-start = ((), (), s32[]{:S(2)}) async-start(), calls=%async_computation.7 | async-start | bytes 2359296 | tf_op jit(solution)/shard_map/all_gather | solution.py:278
  8.9 182.2 %all-gather.29.cloned.1.call-start = ((), (), s32[]{:S(2)}) async-start(), calls=%async_computation.6 | async-start | bytes 4718592 | tf_op jit(solution)/shard_map/all_gather | solution.py:277
  10.3 7.9 %copy-start.12 = (s32[2]{0:T(128)S(1)}, s32[2]{0:T(128)}, u32[]{:S(2)}) copy-start(s32[2]{0:T(128)} %param.21) | copy-start | bytes 28
  10.3 231.1 %all-gather.27.cloned.1.call-start = ((), (), s32[]{:S(2)}) async-start(), calls=%async_computation.5 | async-start | bytes 2359296 | tf_op jit(solution)/shard_map/all_gather | solution.py:278
  11.1 230.3 %all-gather.25.cloned.1.call-start = ((), (), s32[]{:S(2)}) async-start(), calls=%async_computation.4 | async-start | bytes 4718592 | tf_op jit(solution)/shard_map/all_gather | solution.py:277
  11.7 268.6 %all-gather.23.cloned.1.call-start = ((), (), s32[]{:S(2)}) async-start(), calls=%async_computation.3 | async-start | bytes 2359296 | tf_op jit(solution)/shard_map/all_gather | solution.py:278
  12.2 268.0 %all-gather.21.cloned.1.call-start = ((), (), s32[]{:S(2)}) async-start(), calls=%async_computation.2 | async-start | bytes 4718592 | tf_op jit(solution)/shard_map/all_gather | solution.py:277
  12.8 306.7 %all-gather.19.cloned.1.call-start = ((), (), s32[]{:S(2)}) async-start(), calls=%async_computation.1 | async-start | bytes 2359296 | tf_op jit(solution)/shard_map/all_gather | solution.py:278
  13.6 308.3 %all-gather.17.cloned.1.call-start = ((), (), s32[]{:S(2)}) async-start(), calls=%async_computation | async-start | bytes 4718592 | tf_op jit(solution)/shard_map/all_gather | solution.py:277
  13.6 21.7 %collective-permute-start = (bf16[1024,256]{1,0:T(8,128)(2,1)}, bf16[1024,256]{1,0:T(8,128)(2,1)}, u32[]{:S(2)}, u32[]{:S(2)}) collective-permute-start(bf16[1024,256]{1,0:T(8,128)(2,1)} %param.16), channel_id=1, source_target_pairs={{0,1},{1,0},{2,3},{3,2},{4,5},{5,4},{6,7},{7,6},{8,9},{9,8},{10,11... | collective-permute-start | bytes 1572872 | tf_op jit(solution)/shard_map/ppermute | solution.py:232
  16.6 61.0 %collective-permute-start.1 = (bf16[1024,256]{1,0:T(8,128)(2,1)}, bf16[1024,256]{1,0:T(8,128)(2,1)}, u32[]{:S(2)}, u32[]{:S(2)}) collective-permute-start(bf16[1024,256]{1,0:T(8,128)(2,1)} %param.16), channel_id=1, source_target_pairs={{0,2},{1,3},{2,0},{3,1},{4,6},{5,7},{6,4},{7,5},{8,10},{9,11},{10,... | collective-permute-start | bytes 1572872 | tf_op jit(solution)/shard_map/ppermute | solution.py:232
  18.1 60.6 %collective-permute-start.2 = (bf16[1024,256]{1,0:T(8,128)(2,1)}, bf16[1024,256]{1,0:T(8,128)(2,1)}, u32[]{:S(2)}, u32[]{:S(2)}) collective-permute-start(bf16[1024,256]{1,0:T(8,128)(2,1)} %param.16), channel_id=1, source_target_pairs={{0,3},{1,2},{2,1},{3,0},{4,7},{5,6},{6,5},{7,4},{8,11},{9,10},{10,... | collective-permute-start | bytes 1572872 | tf_op jit(solution)/shard_map/ppermute | solution.py:232
  21.9 6.5 %copy-start.9 = (s32[2,16]{1,0:T(2,128)S(1)}, s32[2,16]{1,0:T(2,128)}, u32[]{:S(2)}) copy-start(s32[2,16]{1,0:T(2,128)} %param.20) | copy-start | bytes 388
  26.3 62.9 %collective-permute-start.3 = (bf16[512,1024]{1,0:T(8,128)(2,1)}, bf16[512,1024]{1,0:T(8,128)(2,1)S(1)}, u32[]{:S(2)}, u32[]{:S(2)}) collective-permute-start(bf16[512,1024]{1,0:T(8,128)(2,1)} %get-tuple-element.22), channel_id=1, source_target_pairs={{0,1},{1,0},{2,3},{3,2},{4,5},{5,4},{6,7},{7,6},{8,9},{9,8},{10,11... | collective-permute-start | bytes 3145736 | tf_op jit(solution)/shard_map/ppermute | solution.py:232
  28.3 45.6 %collective-permute-start.4 = (bf16[256,1024]{1,0:T(8,128)(2,1)}, bf16[256,1024]{1,0:T(8,128)(2,1)}, u32[]{:S(2)}, u32[]{:S(2)}) collective-permute-start(bf16[256,1024]{1,0:T(8,128)(2,1)} %param.18), channel_id=1, source_target_pairs={{0,1},{1,0},{2,3},{3,2},{4,5},{5,4},{6,7},{7,6},{8,9},{9,8},{10,11... | collective-permute-start | bytes 1572872 | tf_op jit(solution)/shard_map/ppermute | solution.py:232
  30.4 1.8 copy-start.1
  33.5 3.8 copy-start.2
  35.3 50.6 %collective-permute-start.5 = (bf16[256,1024]{1,0:T(8,128)(2,1)}, bf16[256,1024]{1,0:T(8,128)(2,1)S(1)}, u32[]{:S(2)}, u32[]{:S(2)}) collective-permute-start(bf16[256,1024]{1,0:T(8,128)(2,1)} %param.18), channel_id=1, source_target_pairs={{0,2},{1,3},{2,0},{3,1},{4,6},{5,7},{6,4},{7,5},{8,10},{9,11},{10,... | collective-permute-start | bytes 1572872 | tf_op jit(solution)/shard_map/ppermute | solution.py:232
  73.8 14.3 %collective-permute-start.6 = (bf16[256,1024]{1,0:T(8,128)(2,1)}, bf16[256,1024]{1,0:T(8,128)(2,1)}, u32[]{:S(2)}, u32[]{:S(2)}) collective-permute-start(bf16[256,1024]{1,0:T(8,128)(2,1)} %param.18), channel_id=1, source_target_pairs={{0,3},{1,2},{2,1},{3,0},{4,7},{5,6},{6,5},{7,4},{8,11},{9,10},{10,... | collective-permute-start | bytes 1572872 | tf_op jit(solution)/shard_map/ppermute | solution.py:232
  79.9 1.3 copy-start.3
  89.2 39.4 %copy-start = (bf16[1024,1024]{1,0:T(8,128)(2,1)}, bf16[1024,1024]{1,0:T(8,128)(2,1)S(1)}, u32[]{:S(2)}) copy-start(bf16[1024,1024]{1,0:T(8,128)(2,1)S(1)} %constant_dynamic-update-slice_fusion.w_ref) | copy-start | bytes 6291460
  89.4 1.5 copy-start.4
  128.6 17.1 %copy-start.7 = (f32[512,8]{0,1:T(8,128)S(1)}, f32[512,8]{0,1:T(8,128)}, u32[]{:S(2)}) copy-start(f32[512,8]{0,1:T(8,128)} %param.23) | copy-start | bytes 49156
  128.6 17.1 %copy-start.8 = (s32[512,8]{0,1:T(8,128)S(1)}, s32[512,8]{0,1:T(8,128)}, u32[]{:S(2)}) copy-start(s32[512,8]{0,1:T(8,128)} %param.22) | copy-start | bytes 49156
  133.5 66.6 %collective-permute-start.7 = (bf16[512,1024]{1,0:T(8,128)(2,1)}, bf16[512,1024]{1,0:T(8,128)(2,1)S(1)}, u32[]{:S(2)}, u32[]{:S(2)}) collective-permute-start(bf16[512,1024]{1,0:T(8,128)(2,1)} %get-tuple-element.24.x_ref), channel_id=1, source_target_pairs={{0,1},{1,0},{2,3},{3,2},{4,5},{5,4},{6,7},{7,6},{8,9},{9,8},{10,11... | collective-permute-start | bytes 3145736 | tf_op jit(solution)/shard_map/ppermute | solution.py:232
  145.9 27.6 %collective-permute-start.8 = (f32[512,32]{1,0:T(8,128)S(1)}, f32[512,32]{1,0:T(8,128)S(1)}, u32[]{:S(2)}, u32[]{:S(2)}) collective-permute-start(f32[512,32]{1,0:T(8,128)S(1)} %copy.23), channel_id=1, source_target_pairs={{0,1},{1,0},{2,3},{3,2},{4,5},{5,4},{6,7},{7,6},{8,9},{9,8},{10,11... | collective-permute-start | bytes 196616 | tf_op jit(solution)/shard_map/ppermute | solution.py:232
  146.0 42.4 %collective-permute-start.10 = (f32[512,32]{1,0:T(8,128)S(1)}, f32[512,32]{1,0:T(8,128)S(1)}, u32[]{:S(2)}, u32[]{:S(2)}) collective-permute-start(f32[512,32]{1,0:T(8,128)S(1)} %copy.23), channel_id=1, source_target_pairs={{0,2},{1,3},{2,0},{3,1},{4,6},{5,7},{6,4},{7,5},{8,10},{9,11},{10,... | collective-permute-start | bytes 196616 | tf_op jit(solution)/shard_map/ppermute | solution.py:232
  168.8 21.0 %collective-permute-start.12 = (f32[512,32]{1,0:T(8,128)S(1)}, f32[512,32]{1,0:T(8,128)S(1)}, u32[]{:S(2)}, u32[]{:S(2)}) collective-permute-start(f32[512,32]{1,0:T(8,128)S(1)} %copy.23), channel_id=1, source_target_pairs={{0,3},{1,2},{2,1},{3,0},{4,7},{5,6},{6,5},{7,4},{8,11},{9,10},{10,... | collective-permute-start | bytes 196616 | tf_op jit(solution)/shard_map/ppermute | solution.py:232
  170.2 4.6 %copy-start.10 = (bf16[512,1024]{1,0:T(8,128)(2,1)S(1)}, bf16[512,1024]{1,0:T(8,128)(2,1)}, u32[]{:S(2)}) copy-start(bf16[512,1024]{1,0:T(8,128)(2,1)} %get-tuple-element.24.x_ref) | copy-start | bytes 3145732
  170.2 53.7 %collective-permute-start.9 = (bf16[512,1024]{1,0:T(8,128)(2,1)}, bf16[512,1024]{1,0:T(8,128)(2,1)}, u32[]{:S(2)}, u32[]{:S(2)}) collective-permute-start(bf16[512,1024]{1,0:T(8,128)(2,1)} %get-tuple-element.24.x_ref), channel_id=1, source_target_pairs={{0,2},{1,3},{2,0},{3,1},{4,6},{5,7},{6,4},{7,5},{8,10},{9,11},{10,... | collective-permute-start | bytes 3145736 | tf_op jit(solution)/shard_map/ppermute | solution.py:232
  174.8 57.9 %collective-permute-start.11 = (bf16[512,1024]{1,0:T(8,128)(2,1)S(1)}, bf16[512,1024]{1,0:T(8,128)(2,1)}, u32[]{:S(2)}, u32[]{:S(2)}) collective-permute-start(bf16[512,1024]{1,0:T(8,128)(2,1)S(1)} %copy-done.10), channel_id=1, source_target_pairs={{0,3},{1,2},{2,1},{3,0},{4,7},{5,6},{6,5},{7,4},{8,11},{9,10},{10,... | collective-permute-start | bytes 3145736 | tf_op jit(solution)/shard_map/ppermute | solution.py:232
  200.1 1.0 copy-start.11
  331.1 31.2 %collective-permute-start.13 = (bf16[512,1024]{1,0:T(8,128)(2,1)}, bf16[512,1024]{1,0:T(8,128)(2,1)S(1)}, u32[]{:S(2)}, u32[]{:S(2)}) collective-permute-start(bf16[512,1024]{1,0:T(8,128)(2,1)} %shard_map.144), channel_id=1, source_target_pairs={{0,1},{1,0},{2,3},{3,2},{4,5},{5,4},{6,7},{7,6},{8,9},{9,8},{10,11... | collective-permute-start | bytes 3145736 | tf_op jit(solution)/shard_map/ppermute | solution.py:232
  341.8 47.7 %collective-permute-start.14 = (bf16[512,1024]{1,0:T(8,128)(2,1)}, bf16[512,1024]{1,0:T(8,128)(2,1)S(1)}, u32[]{:S(2)}, u32[]{:S(2)}) collective-permute-start(bf16[512,1024]{1,0:T(8,128)(2,1)} %shard_map.145), channel_id=1, source_target_pairs={{0,2},{1,3},{2,0},{3,1},{4,6},{5,7},{6,4},{7,5},{8,10},{9,11},{10,... | collective-permute-start | bytes 3145736 | tf_op jit(solution)/shard_map/ppermute | solution.py:232
  352.5 37.0 %collective-permute-start.15 = (bf16[512,1024]{1,0:T(8,128)(2,1)}, bf16[512,1024]{1,0:T(8,128)(2,1)S(1)}, u32[]{:S(2)}, u32[]{:S(2)}) collective-permute-start(bf16[512,1024]{1,0:T(8,128)(2,1)} %shard_map.146), channel_id=1, source_target_pairs={{0,3},{1,2},{2,1},{3,0},{4,7},{5,6},{6,5},{7,4},{8,11},{9,10},{10,... | collective-permute-start | bytes 3145736 | tf_op jit(solution)/shard_map/ppermute | solution.py:232
  353.0 36.5 %copy-start.6 = (bf16[512,1024]{1,0:T(8,128)(2,1)S(1)}, bf16[512,1024]{1,0:T(8,128)(2,1)}, u32[]{:S(2)}) copy-start(bf16[512,1024]{1,0:T(8,128)(2,1)} %get-tuple-element.23) | copy-start | bytes 3145732
Sparse Core Ops, SparseCore 0:
  9.0 31.7 all-gather.30
  42.5 46.6 all-gather.28
  90.8 27.8 all-gather.26
  120.1 46.6 all-gather.24
  168.2 27.8 all-gather.22
  197.5 46.6 all-gather.20
  245.8 27.8 all-gather.18
  275.2 46.6 all-gather.16
